TPU v7x, 512 devices: a whole 4x8x8 slice. The times are simulated.
512 devices in a mesh: dp: 32 (over y, x), seq: 16 (over z, core).
Axes of the slice: x: 4, y: 8, z: 8, core: 2. Of those that a mesh axis runs over, the one named last changes fastest.
Arguments:
- tokens: bfloat16 [32, 2048, 2048], P('dp', 'seq'), may hold values from -24 to 24
- qk_weight: bfloat16 [2048, 256], replicated, may hold values from -0.125 to 0.125
- values: bfloat16 [32, 2048, 1024], P('dp', 'seq'), may hold values from -6 to 6
- cotangent: bfloat16 [32, 2048, 1024], P('dp', 'seq'), may hold values from -6 to 6
- key_span: bfloat16 [32, 16, 8, 273, 128], P('dp', 'seq'), may hold values from -96 to 96
- key_span_norm: float32 [32, 16, 8, 273], P('dp', 'seq'), as said below
- query_span: bfloat16 [32, 16, 8, 273, 128], P('dp', 'seq'), may hold values from -0.4375 to 0.4375
- query_span_norm: float32 [32, 16, 8, 273], P('dp', 'seq'), may hold values from -0.4375 to 0.4375
Outputs:
- token_grad: bfloat16 [32, 2048, 2048], P('dp', 'seq')
- value_grad: bfloat16 [32, 2048, 1024], P('dp', 'seq')
- weight_grad: float32 [2048, 256], P('seq')
Inputs may be any that keep to these rules, and one draw needn't show every extreme that they name: Each head's row is a positive combination of phi of head vectors, so phi(u) . key_span_norm is positive for every u.
All inputs are finite; a program needn't handle non-finite values.
Results may differ from a plain program's by a relative error of at most 0.0072.
Values sent between devices are 32-bit elements; how exact they have to be, the bound alone decides.
A program may use at most 128 MiB of HBM per device.

v0:
```python
import math

import jax
import jax.numpy as jnp
from jax import lax
from jax.sharding import PartitionSpec as P

D = 2048
H = 8
FD = 16
DV = 128


highest = lax.Precision.HIGHEST


def prefix(value, axis, join, neutral, backward):
    count, mine = (lax.axis_size(axis), lax.axis_index(axis))
    pieces = jax.tree.map(lambda part: lax.all_gather(part, axis), value)
    if backward:
        pieces = jax.tree.map(lambda part: part[::-1], pieces)
        mine = count - 1 - mine
    so_far = jax.tree.map(
        lambda part, zero: jnp.full_like(part, 0) + jnp.asarray(zero, part.dtype), value, neutral
    )

    def lap(position, so_far):
        longer = join(so_far, jax.tree.map(lambda part: part[position], pieces))
        return jax.tree.map(lambda new, old: jnp.where(position < mine, new, old), longer, so_far)

    return lax.fori_loop(0, count - 1, lap, so_far)


def taylor_features(inputs):
    head_count, feat_width, row_count = inputs.shape
    outer_prod = (inputs[:, :, None, :] * inputs[:, None, :, :]).reshape(
        head_count, feat_width * feat_width, row_count
    )
    ones_row = jnp.ones((head_count, 1, row_count), jnp.float32)
    joined = jnp.concatenate(
        [ones_row, inputs / feat_width**0.25, outer_prod / math.sqrt(2.0 * feat_width)], 1
    )
    return joined.astype(jnp.bfloat16)


def feature_grad(inputs, upstream):
    head_count, feat_width, row_count = inputs.shape
    linear = upstream[:, 1 : 1 + feat_width] / feat_width**0.25
    outer_prod = upstream[:, 1 + feat_width :].reshape(
        head_count, feat_width, feat_width, row_count
    )
    left_part = jnp.einsum("habt,hbt->hat", outer_prod, inputs, precision=highest)
    right_part = jnp.einsum("habt,hat->hbt", outer_prod, inputs, precision=highest)
    return linear + (left_part + right_part) / math.sqrt(2.0 * feat_width)


def add_pair(earlier, following):
    return (earlier[0] + following[0], earlier[1] + following[1])


def on_device(
    tokens, qk_weight, values, cotangent, key_span, key_span_norm, query_span, query_span_norm
):
    activations = tokens[0]
    value_rows = values[0]
    cot_rows = cotangent[0]
    span_keys = key_span[0, 0].astype(jnp.float32)
    span_key_norm = key_span_norm[0, 0]
    span_queries = query_span[0, 0].astype(jnp.float32)
    span_query_norm = query_span_norm[0, 0]
    row_count = activations.shape[0]
    split_col = H * FD
    projected = jnp.dot(activations, qk_weight, preferred_element_type=jnp.float32).astype(
        jnp.bfloat16
    )
    query_rows = projected[:, :split_col].reshape(row_count, H, FD)
    key_rows = projected[:, split_col:].reshape(row_count, H, FD)
    value_heads = value_rows.reshape(row_count, H, DV)
    cot_heads = cot_rows.reshape(row_count, H, DV)
    query_t = query_rows.astype(jnp.float32).transpose(1, 2, 0)
    key_t = key_rows.astype(jnp.float32).transpose(1, 2, 0)
    phi_query = taylor_features(query_t)
    phi_keys = taylor_features(key_t)
    scores = jnp.einsum(
        "thf,shf->hts", query_rows, key_rows, preferred_element_type=jnp.float32
    ) / math.sqrt(FD)
    causal = lax.broadcasted_iota(jnp.int32, (row_count, row_count), 0) >= lax.broadcasted_iota(
        jnp.int32, (row_count, row_count), 1
    )
    weights = jnp.where(causal, 1.0 + scores + 0.5 * scores * scores, 0.0)
    weights_low = weights.astype(jnp.bfloat16)
    state_zero = jnp.zeros((H, 1 + FD + FD * FD, DV), jnp.float32)
    norm_zero = jnp.zeros((H, 1 + FD + FD * FD), jnp.float32)
    local_state = jnp.einsum(
        "hft,thd->hfd", phi_keys, value_heads, preferred_element_type=jnp.float32
    )
    local_norm = jnp.sum(phi_keys.astype(jnp.float32), axis=2)
    earlier_state, earlier_norm = prefix(
        (local_state + span_keys, local_norm + span_key_norm),
        "seq",
        add_pair,
        (state_zero, norm_zero),
        False,
    )
    prefix_state = earlier_state + span_keys
    prefix_norm = earlier_norm + span_key_norm
    prefix_low = prefix_state.astype(jnp.bfloat16)
    numer = jnp.einsum("hft,hfd->thd", phi_query, prefix_low, preferred_element_type=jnp.float32)
    numer = numer + jnp.einsum(
        "hts,shd->thd", weights_low, value_heads, preferred_element_type=jnp.float32
    )
    phi_query_wide = phi_query.astype(jnp.float32)
    denom = (
        jnp.einsum("hft,hf->th", phi_query_wide, prefix_norm, precision=highest)
        + jnp.sum(weights, axis=2).T
    )
    cot_wide = cot_heads.astype(jnp.float32)
    grad_low = (cot_wide / denom[:, :, None]).astype(jnp.bfloat16)
    grad_den = -jnp.sum(cot_wide * numer, axis=2) / (denom * denom)
    query_state = jnp.einsum(
        "hft,thd->hfd", phi_query, grad_low, preferred_element_type=jnp.float32
    )
    query_norm = jnp.einsum("th,hft->hf", grad_den, phi_query_wide, precision=highest)
    suffix_state, suffix_norm = prefix(
        (query_state + span_queries, query_norm + span_query_norm),
        "seq",
        add_pair,
        (state_zero, norm_zero),
        True,
    )
    suffix_low = suffix_state.astype(jnp.bfloat16)
    value_grad = jnp.einsum(
        "hts,thd->shd", weights_low, grad_low, preferred_element_type=jnp.float32
    )
    value_grad = value_grad + jnp.einsum(
        "hft,hfd->thd", phi_keys, suffix_low, preferred_element_type=jnp.float32
    )
    grad_weights = jnp.einsum(
        "thd,shd->hts", grad_low, value_heads, preferred_element_type=jnp.float32
    )
    grad_weights = jnp.where(causal, grad_weights + grad_den.T[:, :, None], 0.0)
    grad_scores = (grad_weights * (1.0 + scores) / math.sqrt(FD)).astype(jnp.bfloat16)
    query_inner = jnp.einsum(
        "hts,shf->thf", grad_scores, key_rows, preferred_element_type=jnp.float32
    )
    key_inner = jnp.einsum(
        "hts,thf->shf", grad_scores, query_rows, preferred_element_type=jnp.float32
    )
    dphi_query = jnp.einsum(
        "thd,hfd->hft", grad_low, prefix_low, preferred_element_type=jnp.float32
    )
    dphi_query = dphi_query + grad_den.T[:, None, :] * prefix_norm[:, :, None]
    dphi_keys = jnp.einsum(
        "thd,hfd->hft", value_heads, suffix_low, preferred_element_type=jnp.float32
    )
    dphi_keys = dphi_keys + suffix_norm[:, :, None]
    dquery = query_inner + feature_grad(query_t, dphi_query).transpose(2, 0, 1)
    dkey = key_inner + feature_grad(key_t, dphi_keys).transpose(2, 0, 1)
    dprojected = jnp.concatenate(
        [dquery.reshape(row_count, split_col), dkey.reshape(row_count, split_col)], 1
    ).astype(jnp.bfloat16)
    token_grad = lax.dot_general(
        dprojected, qk_weight, (((1,), (1,)), ((), ())), preferred_element_type=jnp.float32
    ).astype(jnp.bfloat16)
    term_rows = D // lax.axis_size("seq")
    doc_count = lax.axis_size("dp")
    grad_term = lax.dot_general(
        activations, dprojected, (((0,), (0,)), ((), ())), preferred_element_type=jnp.float32
    )
    total_grad = lax.psum(grad_term, ("dp", "seq"))
    weight_grad = (
        lax.dynamic_slice_in_dim(total_grad, lax.axis_index("seq") * term_rows, term_rows, 0)
        / doc_count
    )
    return (
        token_grad[None],
        value_grad.reshape(row_count, H * DV).astype(jnp.bfloat16)[None],
        weight_grad,
    )


def solution(mesh):
    in_specs = (
        P("dp", "seq", None),
        P(),
        P("dp", "seq", None),
        P("dp", "seq", None),
        P("dp", "seq", None, None, None),
        P("dp", "seq", None, None),
        P("dp", "seq", None, None, None),
        P("dp", "seq", None, None),
    )
    out_specs = (P("dp", "seq", None), P("dp", "seq", None), P("seq", None))
    return jax.shard_map(
        on_device, mesh=mesh, in_specs=in_specs, out_specs=out_specs, check_vma=False
    )
```

profile of v0, /device:TPU:1, one launch (start us, length us, event | category | flops | bytes accessed | tf_op | source)
XLA Modules:
  0.0 640.0 jit_solution(1294393865064413984)
XLA Ops:
  7.2 1.2 copy-done
  8.4 1.3 convolution_convert_fusion.1
  11.4 1.2 copy.57
  15.2 26.7 %all_gather.24 = f32[16,8,273]{2,1,0:T(8,128)} all-gather(f32[1,8,273]{2,1,0:T(8,128)S(1)} %bitcast_add_fusion.2), channel_id=1, replica_groups=mesh['dp'=32,'seq'=16] {'seq'}, dimensions={0}, use_global_device_ids=true | all-gather | bytes 148512 | tf_op jit(solution)/shard_map/all_gather | solution.py:19
  43.1 1.1 fusion.15
  44.1 86.0 %all-gather.6.cloned.1.call-done = f32[128,273,128]{2,0,1:T(8,128)} async-done(((f32[8,273,128]{2,0,1:T(8,128)}), f32[128,273,128]{2,0,1:T(8,128)}) %all-gather.6.cloned.1.call-update) | async-done | bytes 17891344 | tf_op jit(solution)/shard_map/all_gather | solution.py:19
  130.1 38.8 %while.32 = (s32[]{:T(128)}, f32[8,273,128]{2,1,0:T(8,128)S(1)}, f32[8,273]{1,0:T(8,128)S(1)}, s32[]{:T(128)}, f32[16,8,273,128]{3,1,0,2:T(8,128)}, /*index=5*/f32[16,8,273]{2,1,0:T(8,128)}, s32[]{:T(128)}, s32[]{:T(128)}) while((s32[]{:T(128)}, f32[8,273,128]{2,1,0:T(8,128)S(1)}, f32[8,273]{1,0:T(8,128)S(1)}, s32[]{:T(128)}, ...), condition=%wide.region_2.3_spmd.clone, body=%wide.region_1.2_spmd.clone.sunk | while | flops 845212 | bytes 5617363 | solution.py:31
  130.1 1.3 constant_dynamic-slice_fusion.2
  132.7 1.3 constant_dynamic-slice_fusion.2
  135.3 1.3 constant_dynamic-slice_fusion.2
  137.9 1.3 constant_dynamic-slice_fusion.2
  140.5 1.3 constant_dynamic-slice_fusion.2
  143.0 1.3 constant_dynamic-slice_fusion.2
  145.6 1.3 constant_dynamic-slice_fusion.2
  148.2 1.3 constant_dynamic-slice_fusion.2
  150.8 1.3 constant_dynamic-slice_fusion.2
  153.4 1.3 constant_dynamic-slice_fusion.2
  156.0 1.3 constant_dynamic-slice_fusion.2
  158.6 1.3 constant_dynamic-slice_fusion.2
  161.1 1.3 constant_dynamic-slice_fusion.2
  163.7 1.3 constant_dynamic-slice_fusion.2
  166.3 1.3 constant_dynamic-slice_fusion.2
  168.9 1.8 convolution_bitcast_fusion.2
  172.7 1.2 copy.70
  175.3 16.9 %all-gather.2 = f32[128,273]{1,0:T(8,128)S(1)} all-gather(f32[8,273]{1,0:T(8,128)S(1)} %bitcast_add_fusion), channel_id=4, replica_groups=mesh['dp'=32,'seq'=16] {'seq'}, dimensions={0}, use_global_device_ids=true | all-gather | bytes 148512 | tf_op jit(solution)/shard_map/all_gather | solution.py:19
  192.9 1.5 convolution_add_fusion.2
  196.9 87.8 %all-gather.8.cloned.1.call-done = f32[128,273,128]{2,0,1:T(8,128)} async-done(((f32[8,273,128]{2,0,1:T(8,128)}), f32[128,273,128]{2,0,1:T(8,128)}) %all-gather.8.cloned.1.call-update) | async-done | bytes 17891344 | tf_op jit(solution)/shard_map/all_gather | solution.py:19
  284.7 18.9 %copy.71 = f32[16,8,273,128]{3,2,1,0:T(8,128)} copy(f32[16,8,273,128]{3,1,0,2:T(8,128)} %bitcast.139) | data formatting | bytes 35782656 | tf_op jit(solution)/shard_map/all_gather | solution.py:19
  303.5 12.4 %rev.6 = f32[16,8,273,128]{3,2,1,0:T(8,128)} reverse(f32[16,8,273,128]{3,2,1,0:T(8,128)} %copy.71), dimensions={0} | reverse | bytes 35782656 | tf_op jit(solution)/shard_map/rev | solution.py:21
  315.9 33.9 %while.33 = (s32[]{:T(128)}, f32[8,273,128]{2,1,0:T(8,128)S(1)}, f32[8,273]{1,0:T(8,128)S(1)}, s32[]{:T(128)}, f32[16,8,273,128]{3,2,1,0:T(8,128)}, /*index=5*/f32[16,8,273]{2,1,0:T(8,128)}, s32[]{:T(128)}, s32[]{:T(128)}) while((s32[]{:T(128)}, f32[8,273,128]{2,1,0:T(8,128)S(1)}, f32[8,273]{1,0:T(8,128)S(1)}, s32[]{:T(128)}, ...), condition=%wide.region_6.7_spmd.clone, body=%wide.region_5.6_spmd.clone.sunk | while | flops 845212 | bytes 3380947 | solution.py:31
  315.9 1.5 add_select_fusion.11
  318.2 1.5 add_select_fusion.11
  320.5 1.5 add_select_fusion.11
  322.7 1.5 add_select_fusion.11
  325.0 1.5 add_select_fusion.11
  327.3 1.5 add_select_fusion.11
  329.5 1.5 add_select_fusion.11
  331.8 1.5 add_select_fusion.11
  334.0 1.5 add_select_fusion.11
  336.3 1.5 add_select_fusion.11
  338.6 1.5 add_select_fusion.11
  340.8 1.5 add_select_fusion.11
  343.1 1.5 add_select_fusion.11
  345.4 1.5 add_select_fusion.11
  347.6 1.5 add_select_fusion.11
  352.1 1.7 convolution_bitcast_fusion
  356.7 1.3 fusion
  358.0 273.8 %all-reduce.2.cloned.1.call-done = f32[2048,256]{0,1:T(8,128)} async-done(((f32[2048,256]{0,1:T(8,128)}), f32[2048,256]{0,1:T(8,128)}) %all-reduce.2.cloned.1.call-update) | async-done | bytes 2097168 | tf_op jit(solution)/shard_map/psum | solution.py:170
  (160 shorter events, 47.9 us)
Async XLA Ops:
  7.2 1.2 copy-start
  7.2 2.9 copy-start.24
  7.2 122.9 %all-gather.6.cloned.1.call-start = ((), (), s32[]{:S(2)}) async-start(), calls=%async_computation.1 | async-start | bytes 19009536 | tf_op jit(solution)/shard_map/all_gather | solution.py:19
  9.8 1.1 copy-start.8
  9.9 164.1 %copy-start.12 = (bf16[128,128]{0,1:T(8,128)(2,1)}, bf16[128,128]{0,1:T(8,128)(2,1)S(1)}, u32[]{:S(2)}) copy-start(bf16[128,128]{0,1:T(8,128)(2,1)S(1)} %copy.53) | copy-start | bytes 98308
  9.9 4.5 copy-start.21
  10.1 4.4 copy-start.4
  10.2 1.2 copy-start.6
  10.2 31.8 %copy-start.29 = (bf16[273]{0:T(512)(128)(2,1)}, bf16[273]{0:T(512)(128)(2,1)S(1)}, u32[]{:S(2)}) copy-start(bf16[273]{0:T(512)(128)(2,1)S(1)} %pad.5.clone) | copy-start | bytes 1642
  12.6 0.9 copy-start.23
  12.6 2.5 copy-start.28
  12.6 272.1 %all-gather.8.cloned.1.call-start = ((), (), s32[]{:S(2)}) async-start(), calls=%async_computation.2 | async-start | bytes 19009536 | tf_op jit(solution)/shard_map/all_gather | solution.py:19
  41.8 129.3 %copy-start.25 = (pred[128,128]{0,1:T(8,128)(4,1)}, pred[128,128]{0,1:T(8,128)(4,1)S(1)}, u32[]{:S(2)}) copy-start(pred[128,128]{0,1:T(8,128)(4,1)S(1)} %iota_compare_fusion) | copy-start | bytes 49156
  168.9 1.9 copy-start.2
  168.9 2.3 copy-start.3
  168.9 2.3 copy-start.7
  168.9 2.2 copy-start.10
  171.2 1.1 copy-start.16
  173.9 1.4 copy-start.31
  173.9 457.9 %all-reduce.2.cloned.1.call-start = ((), (), s32[]{:S(2)}) async-start(), calls=%async_computation | async-start | bytes 4194304 | tf_op jit(solution)/shard_map/psum | solution.py:170
  174.0 20.4 %copy-start.15 = (f32[8,128,16]{1,2,0:T(8,128)}, f32[8,128,16]{1,2,0:T(8,128)S(1)}, u32[]{:S(2)}) copy-start(f32[8,128,16]{1,2,0:T(8,128)S(1)} %bitcast_convert_fusion.1) | copy-start | bytes 196612
  194.8 1.1 copy-start.11
  194.8 1.1 copy-start.26
  194.8 1.3 copy-start.13
  303.5 12.4 %copy-start.1 = (f32[8,273,128]{2,1,0:T(8,128)S(1)}, f32[8,273,128]{2,1,0:T(8,128)}, u32[]{:S(2)}) copy-start(f32[8,273,128]{2,1,0:T(8,128)} %custom-call.2) | copy-start | bytes 3354628
  349.9 0.8 copy-start.14
  351.1 1.0 copy-start.9
  351.1 1.0 copy-start.17
  351.4 2.4 copy-start.19
  353.8 0.7 copy-start.27
  353.9 1.0 copy-start.5
  353.9 1.0 copy-start.22
  354.6 0.7 copy-start.30
  355.3 1.4 copy-start.18
  355.3 1.4 copy-start.20
Sparse Core Ops, SparseCore 0:
  12.7 117.3 all-gather.5
  174.1 110.5 all-gather.7
  354.0 277.7 all-reduce.1
where the time goes:
time: 643 us; the launch traced here: 640 us
  waiting for transfers between devices  448 us (70%)
  local copies, waits for them, and re-layouts  62.4 us (10%)
  other arithmetic  58.2 us (9%)
  blocking collectives  43.6 us (7%)
  between operations  14.3 us (2%)
  matrix products  13.7 us (2%)
    psum x1, waiting for transfers between devices, on_device(): total_grad = lax.psum(grad_term, ('dp', 'seq'))  274 us
    all_gather x2, waiting for transfers between devices, prefix(): pieces = jax.tree.map(lambda part: lax.all_gather(part, axis), value)  174 us
    select_n x60, other arithmetic, lap(): jnp.where(position < mine, new, old)  52.7 us
    all_gather x2, blocking collectives, prefix(): pieces = jax.tree.map(lambda part: lax.all_gather(part, axis), value)  43.6 us
    dynamic_slice x15, local copies, waits for them, and re-layouts, lap(): longer = join(so_far, jax.tree.map(lambda part: part[position], pieces))  19.8 us
    all_gather x1, local copies, waits for them, and re-layouts, prefix(): pieces = jax.tree.map(lambda part: lax.all_gather(part, axis), value)  18.9 us
    rev x2, local copies, waits for them, and re-layouts, prefix(): pieces = jax.tree.map(lambda part: part[::-1], pieces)  13.1 us
  transfers between devices with their start and end apart: 3, of which 3 were waited for; matrix products, arithmetic and copies ran while one was open for 2% of the time, Pallas kernels for 0%

commit v1 on v0

v1 whole, which is shorter than its diff:
```python
import functools
import math

import jax
import jax.numpy as jnp
from jax import lax
from jax.experimental import pallas as pl
from jax.experimental.pallas import tpu as pltpu
from jax.sharding import PartitionSpec as P

H = 8
FD = 16
DV = 128
F = 273
T = 128
R = 160
HALF = H // 2
PAIR = 1.0 / math.sqrt(2.0 * FD)
LINEAR = 1.0 / FD**0.25
f32 = jnp.float32
bf16 = jnp.bfloat16
MESH = pl.DeviceIdType.MESH


def dot(left, right, left_dim=1, right_dim=0):
    return lax.dot_general(
        left, right, (((left_dim,), (right_dim,)), ((), ())), preferred_element_type=f32
    )


def split(x, parts):
    out = []
    for _ in range(parts):
        low = x.astype(bf16)
        out.append(low)
        x = x - low.astype(f32)
    return out


def fold_matrix():
    row = lax.broadcasted_iota(jnp.int32, (R, F), 0)
    col = lax.broadcasted_iota(jnp.int32, (R, F), 1)
    pair = col - 17
    a, b = (pair >> 4) & 15, pair & 15
    d = (b - a) & 15
    target = jnp.where(d <= 7, d * 16 + a, (16 - d) * 16 + b)
    target = jnp.where(d == 8, 144 + jnp.minimum(a, b), target)
    target = jnp.where(col <= 16, 127 + col, target)
    target = jnp.where(col == 0, 152, target)
    return jnp.where(row == target, 1.0, 0.0).astype(bf16)


def twice(shape, dim):
    row = lax.broadcasted_iota(jnp.int32, shape, dim)
    doubled = ((row >= 16) & (row < 128)) | ((row >= 144) & (row < 152))
    return jnp.where(doubled, 2.0, 1.0)


def features(u):
    rows = [u * (u if d == 0 else pltpu.roll(u, FD - d, 0)) * PAIR for d in range(8)]
    rows.append(u * LINEAR)
    rows.append(u[:8] * u[8:] * PAIR)
    rows.append(jnp.where(lax.broadcasted_iota(jnp.int32, (8, T), 0) == 0, 1.0, 0.0))
    return jnp.concatenate(rows, 0)


def feature_grad(u, y):
    acc = 2.0 * y[:16] * u
    for d in range(1, 8):
        part = y[16 * d : 16 * d + 16]
        acc = acc + part * pltpu.roll(u, FD - d, 0) + pltpu.roll(part * u, d, 0)
    last = y[144:152]
    acc = acc + jnp.concatenate([last * u[8:], last * u[:8]], 0)
    return y[128:144] * LINEAR + acc * PAIR


def kernel(
    sizes,
    tok_h, w_h, val_h, cot_h, ks_h, kn_h, qs_h, qn_h,
    tg_h, vg_h, wg_h,
    tok, w, val, cot, ks, kn, qs, qn,
    tg, vg, wg,
    qt, kt, phi_q, phi_k, phi_qt, phi_kt, fold,
    score, a_low, value_part, den, g_low, gs, p_low, norm_t,
    span, contrib, other, chain_in, chain_out, pre, pre_out,
    norm_own, norm_in, gden_t, dproj_t,
    term, core_in, z_out, z_in, y_out, y_in, x_in, y_all,
    in_sem, out_sem,
    norm_send, norm_recv, other_send, other_recv, chain_send, chain_recv, pre_send, pre_recv,
    core_send, core_recv, z_send, z_recv, y_send, y_recv, x_send, x_recv, all_send, all_recv,
):
    ns, ny, nx, d_model = sizes
    nz = ns // 2
    rows = d_model // ns
    piece = rows // ny
    dp = lax.axis_index("dp")
    me = lax.axis_index("seq")
    z, c = me // 2, lax.rem(me, 2)
    y, x = dp // nx, lax.rem(dp, nx)
    mate = 2 * z + (1 - c)

    def seq_peer(step):
        return lax.rem(me + step, ns)

    def z_peer(step):
        return lax.rem(z + step, nz)

    def y_peer(step):
        return lax.rem(y + step, ny)

    def x_peer(step):
        return lax.rem(x + step, nx)

    loads = [
        pltpu.make_async_copy(src, dst, in_sem.at[i])
        for i, (src, dst) in enumerate(
            [(tok_h, tok), (w_h, w), (val_h, val), (ks_h, ks), (kn_h, kn), (cot_h, cot), (qs_h, qs), (qn_h, qn)]
        )
    ]
    for load in loads:
        load.start()

    barrier = pltpu.get_barrier_semaphore()
    for step in range(1, ns):
        pl.semaphore_signal(barrier, inc=1, device_id=(dp, seq_peer(step)), device_id_type=MESH)
    for step in range(1, ny):
        pl.semaphore_signal(barrier, inc=1, device_id=(y_peer(step) * nx + x, me), device_id_type=MESH)
    for step in range(1, nx):
        pl.semaphore_signal(barrier, inc=1, device_id=(y * nx + x_peer(step), me), device_id_type=MESH)

    def remote(src, dst, send, recv, device):
        return pltpu.make_async_remote_copy(
            src_ref=src, dst_ref=dst, send_sem=send, recv_sem=recv, device_id=device, device_id_type=MESH
        )

    def norm_copy(which, step):
        return remote(
            norm_own.at[which], norm_in.at[which, step],
            norm_send.at[which, step], norm_recv.at[which, step], (dp, seq_peer(step)),
        )

    def other_copy(which, k):
        return remote(
            contrib.at[which, (1 - c) * HALF + k], other.at[which, k],
            other_send.at[which, k], other_recv.at[which, k], (dp, mate),
        )

    def chain_copy(which, k):
        target = jnp.clip(z + 1 - 2 * which, 0, nz - 1)
        return remote(
            chain_out.at[which, k], chain_in.at[which, k],
            chain_send.at[which, k], chain_recv.at[which, k], (dp, 2 * target + c),
        )

    def pre_copy(which, k):
        return remote(
            pre_out.at[which, k], pre.at[which, c * HALF + k],
            pre_send.at[which, k], pre_recv.at[which, k], (dp, mate),
        )

    def core_copy(k):
        return remote(
            term.at[2 * k + (1 - c)], core_in.at[k], core_send.at[k], core_recv.at[k], (dp, mate)
        )

    def z_copy(step):
        return remote(
            z_out.at[z_peer(step)], z_in.at[step], z_send.at[step], z_recv.at[step],
            (dp, 2 * z_peer(step) + c),
        )

    def y_copy(step):
        return remote(
            y_out.at[y_peer(step)], y_in.at[step], y_send.at[step], y_recv.at[step],
            (y_peer(step) * nx + x, me),
        )

    def x_copy(step):
        return remote(
            x_in.at[x], x_in.at[x], x_send.at[step], x_recv.at[step], (y * nx + x_peer(step), me)
        )

    def all_copy(step):
        return remote(
            y_all.at[y], y_all.at[y], all_send.at[step], all_recv.at[step],
            (y_peer(step) * nx + x, me),
        )

    coef = twice((R, DV), 0)
    coef_row = twice((H, R), 1)
    head_row = lax.broadcasted_iota(jnp.int32, (H, R), 0)
    fold[...] = fold_matrix()

    def lanes(h):
        return slice(h * DV, (h + 1) * DV)

    def feat(h):
        return slice(h * FD, (h + 1) * FD)

    def fold_norm(value):
        return sum(dot(part, fold[...], 1, 1) for part in split(value, 3))

    loads[0].wait()
    loads[1].wait()
    projected = dot(tok[0], w[...]).astype(bf16)
    qt[...] = projected[:, : H * FD].astype(f32).T
    kt[...] = projected[:, H * FD :].astype(f32).T
    total = jnp.zeros((H, R), f32)
    ones = jnp.ones((H, T), bf16)
    for h in range(H):
        phi = features(kt[feat(h), :])
        phi_k[h] = phi.astype(bf16)
        phi_kt[h] = phi.T.astype(bf16)
        total = jnp.where(head_row == h, dot(ones, phi_k[h], 1, 1), total)
    loads[4].wait()
    own_norm = fold_norm(kn[0, 0])
    norm_own[0] = total * coef_row + own_norm
    pl.semaphore_wait(barrier, ns + ny + nx - 3)
    for step in range(1, ns):
        norm_copy(0, step).start()

    loads[2].wait()
    loads[3].wait()
    for h in range(H):
        span[h] = dot(fold[...], ks[0, 0, h])
        contrib[0, h] = dot(phi_k[h], val[0, :, lanes(h)]) * coef + span[h]
    for k in range(HALF):
        other_copy(0, k).start()

    causal = lax.broadcasted_iota(jnp.int32, (T, T), 0) >= lax.broadcasted_iota(jnp.int32, (T, T), 1)
    head_lane = lax.broadcasted_iota(jnp.int32, (T, H * FD), 1) // FD
    query, key = projected[:, : H * FD], projected[:, H * FD :]
    for h in range(H):
        phi = features(qt[feat(h), :])
        phi_q[h] = phi.astype(bf16)
        phi_qt[h] = phi.T.astype(bf16)
        masked = jnp.where(head_lane == h, query, jnp.zeros_like(query))
        s = dot(masked, key, 1, 1) * (1.0 / math.sqrt(FD))
        score[h] = s
        a = jnp.where(causal, 1.0 + s + 0.5 * s * s, 0.0)
        a_low[h] = a.astype(bf16)
        den[h] = jnp.broadcast_to(jnp.sum(a, axis=1, keepdims=True), (T, DV))

    for step in range(1, ns):
        norm_copy(0, step).wait_recv()
    norm = own_norm
    for step in range(1, ns):
        norm = norm + jnp.where(me >= step, norm_in[0, step], 0.0)
    norm_parts = jnp.concatenate(split(norm, 3), 0)
    two_parts = split(norm, 2)
    norm_t[...] = jnp.concatenate(two_parts + two_parts, 0).astype(f32).T.astype(bf16)

    loads[5].wait()
    loads[6].wait()
    part_lane = lax.broadcasted_iota(jnp.int32, (T, 3 * H), 1) & (H - 1)
    for h in range(H):
        inner = dot(phi_qt[h], norm_parts, 1, 1)
        whole = den[h] + jnp.sum(jnp.where(part_lane == h, inner, 0.0), axis=1, keepdims=True)
        den[h] = whole
        g_low[h] = (cot[0, :, lanes(h)].astype(f32) / whole).astype(bf16)
        contrib[1, h] = dot(phi_q[h], g_low[h]) * coef + dot(fold[...], qs[0, 0, h])
    for k in range(HALF):
        other_copy(1, k).start()
    for h in range(H):
        value_part[h] = dot(a_low[h], val[0, :, lanes(h)])

    ahead = jnp.clip(5 * (nz - 1 - 2 * z) // 4, -HALF, HALF)

    def pass_on(which, k):
        mine = c * HALF + k
        first = jnp.where(which == 0, z == 0, z == nz - 1)
        last = jnp.where(which == 0, z == nz - 1, z == 0)
        other_copy(which, k).wait_recv()

        @pl.when(first)
        def _():
            chain_in[which, k] = jnp.zeros((R, DV), f32)

        @pl.when(jnp.logical_not(first))
        def _():
            chain_copy(which, k).wait_recv()

        before = chain_in[which, k]
        here = contrib[which, mine]
        there = other[which, k]

        @pl.when(jnp.logical_not(last))
        def _():
            chain_out[which, k] = before + (here + there)
            chain_copy(which, k).start()

        second = (c ^ which) == 1
        pre[which, mine] = before + jnp.where(second, there, 0.0)
        pre_out[which, k] = before + jnp.where(second, 0.0, here)
        pre_copy(which, k).start()

    def chain_step(i, carry):
        for which, lag in ((0, jnp.maximum(-ahead, 0)), (1, jnp.maximum(ahead, 0))):
            k = i - lag

            @pl.when((k >= 0) & (k < HALF))
            def _():
                pass_on(which, k)

        return carry

    lax.fori_loop(0, 2 * HALF, chain_step, 0)
    for which in range(2):
        for k in range(HALF):
            pre_copy(which, k).wait_recv()

    lane = lax.broadcasted_iota(jnp.int32, (T, DV), 1)
    gden_all = jnp.zeros((T, DV), f32)
    for h in range(H):
        p_low[h] = (pre[0, h] + span[h]).astype(bf16)
        numer = dot(phi_qt[h], p_low[h]) + value_part[h]
        weighted = jnp.sum(cot[0, :, lanes(h)].astype(f32) * numer, axis=1, keepdims=True)
        gden = -weighted / (den[h] * den[h])
        gden_all = jnp.where(lane == h, gden, gden_all)
        ga = jnp.where(causal, dot(g_low[h], val[0, :, lanes(h)], 1, 1) + gden, 0.0)
        gs[h] = (ga * (1.0 + score[h]) * (1.0 / math.sqrt(FD))).astype(bf16)
    gden_t[...] = gden_all.T[:H]
    gden_parts = jnp.concatenate(split(gden_t[...], 3), 0)
    total = jnp.zeros((H, R), f32)
    for h in range(H):
        every = dot(gden_parts, phi_q[h], 1, 1)
        every = every[:H] + every[H : 2 * H] + every[2 * H :]
        total = jnp.where(head_row == h, every, total)
    loads[7].wait()
    norm_own[1] = total * coef_row + fold_norm(qn[0, 0])
    for step in range(1, ns):
        norm_copy(1, step).start()

    high, low = split(gden_t[...], 2)
    gden_rows = jnp.concatenate([high, high, low, low], 0)
    four_row = lax.broadcasted_iota(jnp.int32, (4 * H, T), 0) & (H - 1)
    for h in range(H):
        only = jnp.where(four_row == h, gden_rows, jnp.zeros_like(gden_rows))
        up = dot(p_low[h], g_low[h], 1, 1) + dot(norm_t[...], only)
        u = qt[feat(h), :]
        dproj_t[feat(h), :] = feature_grad(u, up) + dot(kt[feat(h), :].astype(bf16), gs[h], 1, 1)
    for h in range(H):
        p_low[h] = pre[1, h].astype(bf16)
        vg[0, :, lanes(h)] = (dot(a_low[h], g_low[h], 0, 0) + dot(phi_kt[h], p_low[h])).astype(bf16)
    store_vg = pltpu.make_async_copy(vg, vg_h, out_sem.at[0])
    store_vg.start()

    for step in range(1, ns):
        norm_copy(1, step).wait_recv()
    norm = jnp.zeros((H, R), f32)
    for step in range(1, ns):
        norm = norm + jnp.where(me + (ns - step) < ns, norm_in[1, step], 0.0)
    parts = split(norm, 3)
    norm_t[...] = jnp.concatenate(parts + [jnp.zeros_like(parts[0])], 0).astype(f32).T.astype(bf16)
    for h in range(H):
        only = jnp.where(four_row == h, 1.0, 0.0).astype(bf16)
        up = dot(p_low[h], val[0, :, lanes(h)], 1, 1) + dot(norm_t[...], only)
        u = kt[feat(h), :]
        inner = dot(qt[feat(h), :].astype(bf16), gs[h])
        dproj_t[H * FD + h * FD : H * FD + (h + 1) * FD, :] = feature_grad(u, up) + inner
    dproj = dproj_t[...].T.astype(bf16)

    for k in range(nz):
        chunk = pl.ds(pl.multiple_of((2 * k + 1 - c) * rows, rows), rows)
        term[2 * k + 1 - c] = dot(tok[0, :, chunk], dproj, 0, 0)
        core_copy(k).start()
    for k in range(nz):
        chunk = pl.ds(pl.multiple_of((2 * k + c) * rows, rows), rows)
        term[2 * k + c] = dot(tok[0, :, chunk], dproj, 0, 0)
    for k in range(nz):
        core_copy(k).wait_recv()
    for k in range(nz):
        z_out[k] = term[2 * k + c] + core_in[k]
    for step in range(1, nz):
        z_copy(step).start()

    cols = min(512, d_model)
    for j in range(d_model // cols):
        tg[0, :, j * cols : (j + 1) * cols] = dot(dproj, w[j * cols : (j + 1) * cols, :], 1, 1).astype(bf16)
    store_tg = pltpu.make_async_copy(tg, tg_h, out_sem.at[1])
    store_tg.start()

    acc = z_out[z]
    for step in range(1, nz):
        z_copy(step).wait_recv()
        acc = acc + z_in[step]
    y_out[...] = acc.reshape(ny, piece, 2 * H * FD)
    for step in range(1, ny):
        y_copy(step).start()
    acc = y_out[y]
    for step in range(1, ny):
        y_copy(step).wait_recv()
        acc = acc + y_in[step]
    x_in[x] = acc
    for step in range(1, nx):
        x_copy(step).start()
    for step in range(1, nx):
        source = lax.rem(x + nx - step, nx)
        remote(
            x_in.at[source], x_in.at[source], x_send.at[step], x_recv.at[step],
            (y * nx + x_peer(step), me),
        ).wait_recv()
    acc = x_in[0]
    for j in range(1, nx):
        acc = acc + x_in[j]
    y_all[y] = acc * (1.0 / (ny * nx))
    for step in range(1, ny):
        all_copy(step).start()
    for step in range(1, ny):
        source = lax.rem(y + ny - step, ny)
        remote(
            y_all.at[source], y_all.at[source], all_send.at[step], all_recv.at[step],
            (y_peer(step) * nx + x, me),
        ).wait_recv()
    wg[...] = y_all[...].reshape(rows, 2 * H * FD)
    store_wg = pltpu.make_async_copy(wg, wg_h, out_sem.at[2])
    store_wg.start()

    for which in range(2):
        for step in range(1, ns):
            norm_copy(which, step).wait_send()
        last = (z == nz - 1) if which == 0 else (z == 0)
        for k in range(HALF):
            other_copy(which, k).wait_send()
            pre_copy(which, k).wait_send()

            @pl.when(jnp.logical_not(last))
            def _():
                chain_copy(which, k).wait_send()

    for k in range(nz):
        core_copy(k).wait_send()
    for step in range(1, nz):
        z_copy(step).wait_send()
    for step in range(1, ny):
        y_copy(step).wait_send()
        all_copy(step).wait_send()
    for step in range(1, nx):
        x_copy(step).wait_send()
    store_vg.wait()
    store_tg.wait()
    store_wg.wait()


def on_device(sizes, tokens, qk_weight, values, cotangent, key_span, key_norm, query_span, query_norm):
    ns, ny, nx, d_model = sizes
    nz = ns // 2
    rows = d_model // ns
    piece = rows // ny
    width = 2 * H * FD
    args = (tokens, qk_weight, values, cotangent, key_span, key_norm, query_span, query_norm)
    out_shape = (
        jax.ShapeDtypeStruct((1, T, d_model), bf16),
        jax.ShapeDtypeStruct((1, T, H * DV), bf16),
        jax.ShapeDtypeStruct((rows, width), f32),
    )
    vmem, dma = pltpu.VMEM, pltpu.SemaphoreType.DMA
    scratch = [vmem(a.shape, a.dtype) for a in args] + [vmem(o.shape, o.dtype) for o in out_shape]
    scratch += [
        vmem((H * FD, T), f32),
        vmem((H * FD, T), f32),
        vmem((H, R, T), bf16),
        vmem((H, R, T), bf16),
        vmem((H, T, R), bf16),
        vmem((H, T, R), bf16),
        vmem((R, F), bf16),
        vmem((H, T, T), f32),
        vmem((H, T, T), bf16),
        vmem((H, T, DV), f32),
        vmem((H, T, DV), f32),
        vmem((H, T, DV), bf16),
        vmem((H, T, T), bf16),
        vmem((H, R, DV), bf16),
        vmem((R, 4 * H), bf16),
        vmem((H, R, DV), f32),
        vmem((2, H, R, DV), f32),
        vmem((2, HALF, R, DV), f32),
        vmem((2, HALF, R, DV), f32),
        vmem((2, HALF, R, DV), f32),
        vmem((2, H, R, DV), f32),
        vmem((2, HALF, R, DV), f32),
        vmem((2, H, R), f32),
        vmem((2, ns, H, R), f32),
        vmem((H, T), f32),
        vmem((width, T), f32),
        vmem((ns, rows, width), f32),
        vmem((nz, rows, width), f32),
        vmem((nz, rows, width), f32),
        vmem((nz, rows, width), f32),
        vmem((ny, piece, width), f32),
        vmem((ny, piece, width), f32),
        vmem((nx, piece, width), f32),
        vmem((ny, piece, width), f32),
        dma((8,)), dma((3,)),
        dma((2, ns)), dma((2, ns)),
        dma((2, HALF)), dma((2, HALF)),
        dma((2, HALF)), dma((2, HALF)),
        dma((2, HALF)), dma((2, HALF)),
        dma((nz,)), dma((nz,)),
        dma((nz,)), dma((nz,)),
        dma((ny,)), dma((ny,)),
        dma((nx,)), dma((nx,)),
        dma((ny,)), dma((ny,)),
    ]
    return pl.pallas_call(
        functools.partial(kernel, sizes),
        out_shape=out_shape,
        in_specs=[pl.BlockSpec(memory_space=pl.ANY)] * 8,
        out_specs=(pl.BlockSpec(memory_space=pl.ANY),) * 3,
        scratch_shapes=scratch,
        compiler_params=pltpu.CompilerParams(
            collective_id=0, has_side_effects=True, vmem_limit_bytes=48 * 1024 * 1024
        ),
    )(*args)


def solution(mesh):
    ns, docs = mesh.shape["seq"], mesh.shape["dp"]
    nx = 4 if docs >= 16 else 2

    def whole(*args):
        sizes = (ns, docs // nx, nx, args[0].shape[2])
        in_specs = (
            P("dp", "seq", None),
            P(),
            P("dp", "seq", None),
            P("dp", "seq", None),
            P("dp", "seq", None, None, None),
            P("dp", "seq", None, None),
            P("dp", "seq", None, None, None),
            P("dp", "seq", None, None),
        )
        out_specs = (P("dp", "seq", None), P("dp", "seq", None), P("seq", None))
        return jax.shard_map(
            functools.partial(on_device, sizes),
            mesh=mesh,
            in_specs=in_specs,
            out_specs=out_specs,
            check_vma=False,
        )(*args)

    return whole
```

time: 643 us -> 115 us (0.18)
  the two profiles are of different devices: /device:TPU:1 before, /device:TPU:16 now
where the time goes in v1:
time: 115 us
  Pallas kernels  109 us (95%)
  local copies, waits for them, and re-layouts  4.71 us (4%)
    pallas_call x1, Pallas kernels, on_device(): pl.pallas_call(functools.partial(kernel, sizes), out_shape=out_shape, in_...  109 us
    unnamed x17, local copies, waits for them, and re-layouts  4.71 us

profile of v1, /device:TPU:16, one launch (start us, length us, event | category | flops | bytes accessed | tf_op | source)
XLA Modules:
  0.0 114.6 jit_solution(12109293819679009143)
XLA Ops:
  0.6 0.0 copy-start
  0.6 1.2 %copy.11.ks_h = bf16[1,1,8,273,128]{4,3,2,1,0:T(8,128)(2,1)S(1)} copy(bf16[1,1,8,273,128]{4,2,3,1,0:T(8,128)(2,1)} %param.12) | data formatting | bytes 1118208 | tf_op args[4]
  1.9 0.0 copy-start.1
  1.9 0.0 copy-start.2
  1.9 0.0 copy-start.3
  1.9 0.0 copy-start.4
  1.9 0.0 copy-start.5
  1.9 1.2 %copy.12.qs_h = bf16[1,1,8,273,128]{4,3,2,1,0:T(8,128)(2,1)S(1)} copy(bf16[1,1,8,273,128]{4,2,3,1,0:T(8,128)(2,1)} %param.14) | data formatting | bytes 1118208 | tf_op args[6]
  3.1 0.0 copy-done
  3.1 0.0 copy-done.1
  3.2 0.0 copy-done.2
  3.2 0.1 copy-done.3
  3.3 0.0 copy-done.4
  3.3 0.0 copy-done.5
  3.3 109.2 %shard_map.103 = (bf16[1,128,2048]{2,1,0:T(8,128)(2,1)S(1)}, bf16[1,128,1024]{2,1,0:T(8,128)(2,1)S(1)}, f32[128,256]{1,0:T(8,128)S(1)}) custom-call(bf16[1,128,2048]{2,1,0:T(8,128)(2,1)S(1)} %copy-done.1, bf16[2048,256]{1,0:T(8,128)(2,1)S(1)} %copy-done, bf16[1,128,1024]{2,1,0:T(8,128)(2,1)S(1)} %copy-done.2, bf16[1,128,1024]{2,1,0:T(8,128)(2,1)S(1)} %copy-done.3, ...), custom_call_target="tpu_custom_call" | custom-call | tf_op jit(solution)/shard_map/pallas_call | solution.py:505
  112.4 0.8 copy.16
  113.2 0.7 copy.17
  113.9 0.7 copy.18
Async XLA Ops:
  0.6 2.5 %copy-start = (bf16[2048,256]{1,0:T(8,128)(2,1)S(1)}, bf16[2048,256]{1,0:T(8,128)(2,1)}, u32[]{:S(2)}) copy-start(bf16[2048,256]{1,0:T(8,128)(2,1)} %w_h.1) | copy-start | bytes 3145732
  1.9 1.3 %copy-start.1 = (bf16[1,128,2048]{2,1,0:T(8,128)(2,1)S(1)}, bf16[1,128,2048]{2,1,0:T(8,128)(2,1)}, u32[]{:S(2)}) copy-start(bf16[1,128,2048]{2,1,0:T(8,128)(2,1)} %tok_h.1) | copy-start | bytes 1572868
  1.9 1.3 %copy-start.2 = (bf16[1,128,1024]{2,1,0:T(8,128)(2,1)S(1)}, bf16[1,128,1024]{2,1,0:T(8,128)(2,1)}, u32[]{:S(2)}) copy-start(bf16[1,128,1024]{2,1,0:T(8,128)(2,1)} %val_h.1) | copy-start | bytes 786436
  1.9 1.4 %copy-start.3 = (bf16[1,128,1024]{2,1,0:T(8,128)(2,1)S(1)}, bf16[1,128,1024]{2,1,0:T(8,128)(2,1)}, u32[]{:S(2)}) copy-start(bf16[1,128,1024]{2,1,0:T(8,128)(2,1)} %cot_h.1) | copy-start | bytes 786436
  1.9 1.4 %copy-start.4 = (f32[1,1,8,273]{3,2,1,0:T(8,128)S(1)}, f32[1,1,8,273]{3,2,1,0:T(8,128)}, u32[]{:S(2)}) copy-start(f32[1,1,8,273]{3,2,1,0:T(8,128)} %kn_h.1) | copy-start | bytes 26212
  1.9 1.3 %copy-start.5 = (f32[1,1,8,273]{3,2,1,0:T(8,128)S(1)}, f32[1,1,8,273]{3,2,1,0:T(8,128)}, u32[]{:S(2)}) copy-start(f32[1,1,8,273]{3,2,1,0:T(8,128)} %qn_h.1) | copy-start | bytes 26212

commit v2 on v1

--- a/solution.py
+++ b/solution.py
@@ -82,25 +82,28 @@
     tg, vg, wg,
     qt, kt, phi_q, phi_k, phi_qt, phi_kt, fold,
     score, a_low, value_part, den, g_low, gs, p_low, norm_t,
-    span, contrib, other, chain_in, chain_out, pre, pre_out,
-    norm_own, norm_in, gden_t, dproj_t,
-    term, core_in, z_out, z_in, y_out, y_in, x_in, y_all,
+    span, contrib, other, pair_out, pair_in, chain_in, chain_out, back_out, back_in, pre, pre_out,
+    row_sum, norm_own, norm_mate, norm_chip, norm_in, gden_t, dproj_t,
+    term, core_in, z_out, z_in, zx_out, zx_in, xs_out, xs_in, xz_out, xz_in, y_part, x_part,
     in_sem, out_sem,
-    norm_send, norm_recv, other_send, other_recv, chain_send, chain_recv, pre_send, pre_recv,
-    core_send, core_recv, z_send, z_recv, y_send, y_recv, x_send, x_recv, all_send, all_recv,
+    mate_send, mate_recv, norm_send, norm_recv, other_send, other_recv, pair_send, pair_recv,
+    chain_send, chain_recv, back_send, back_recv, pre_send, pre_recv,
+    core_send, core_recv, z_send, z_recv, zx_send, zx_recv, xs_send, xs_recv, xz_send, xz_recv,
+    y_send, y_recv, x_send, x_recv,
 ):
     ns, ny, nx, d_model = sizes
     nz = ns // 2
     rows = d_model // ns
-    piece = rows // ny
+    pairs = nz // 2
+    half = rows // 2
+    piece = half // nx
     dp = lax.axis_index("dp")
     me = lax.axis_index("seq")
     z, c = me // 2, lax.rem(me, 2)
     y, x = dp // nx, lax.rem(dp, nx)
+    p, e = z // 2, lax.rem(z, 2)
     mate = 2 * z + (1 - c)
-
-    def seq_peer(step):
-        return lax.rem(me + step, ns)
+    partner = 4 * p + 2 * (1 - e) + c
 
     def z_peer(step):
         return lax.rem(z + step, nz)
@@ -120,23 +123,38 @@
     for load in loads:
         load.start()
 
+    def across_z(step):
+        return (dp, 2 * z_peer(step) + c)
+
+    def across_y(step):
+        return (y_peer(step) * nx + x, me)
+
+    def across_x(step):
+        return (y * nx + x_peer(step), me)
+
     barrier = pltpu.get_barrier_semaphore()
-    for step in range(1, ns):
-        pl.semaphore_signal(barrier, inc=1, device_id=(dp, seq_peer(step)), device_id_type=MESH)
+    pl.semaphore_signal(barrier, inc=1, device_id=(dp, mate), device_id_type=MESH)
+    for step in range(1, nz):
+        pl.semaphore_signal(barrier, inc=1, device_id=across_z(step), device_id_type=MESH)
     for step in range(1, ny):
-        pl.semaphore_signal(barrier, inc=1, device_id=(y_peer(step) * nx + x, me), device_id_type=MESH)
+        pl.semaphore_signal(barrier, inc=1, device_id=across_y(step), device_id_type=MESH)
     for step in range(1, nx):
-        pl.semaphore_signal(barrier, inc=1, device_id=(y * nx + x_peer(step), me), device_id_type=MESH)
+        pl.semaphore_signal(barrier, inc=1, device_id=across_x(step), device_id_type=MESH)
 
     def remote(src, dst, send, recv, device):
         return pltpu.make_async_remote_copy(
             src_ref=src, dst_ref=dst, send_sem=send, recv_sem=recv, device_id=device, device_id_type=MESH
         )
 
+    def mate_copy(which):
+        return remote(
+            norm_own.at[which], norm_mate.at[which], mate_send.at[which], mate_recv.at[which], (dp, mate)
+        )
+
     def norm_copy(which, step):
         return remote(
-            norm_own.at[which], norm_in.at[which, step],
-            norm_send.at[which, step], norm_recv.at[which, step], (dp, seq_peer(step)),
+            norm_chip.at[which], norm_in.at[which, step],
+            norm_send.at[which, step], norm_recv.at[which, step], across_z(step),
         )
 
     def other_copy(which, k):
@@ -145,11 +163,23 @@
             other_send.at[which, k], other_recv.at[which, k], (dp, mate),
         )
 
-    def chain_copy(which, k):
-        target = jnp.clip(z + 1 - 2 * which, 0, nz - 1)
-        return remote(
-            chain_out.at[which, k], chain_in.at[which, k],
-            chain_send.at[which, k], chain_recv.at[which, k], (dp, 2 * target + c),
+    def pair_copy(which, j):
+        return remote(
+            pair_out.at[which, j], pair_in.at[which, j],
+            pair_send.at[which, j], pair_recv.at[which, j], (dp, partner),
+        )
+
+    def chain_copy(which, j):
+        target = jnp.clip(p + 1 - 2 * which, 0, pairs - 1)
+        return remote(
+            chain_out.at[which, j], chain_in.at[which, j],
+            chain_send.at[which, j], chain_recv.at[which, j], (dp, 4 * target + 2 * e + c),
+        )
+
+    def back_copy(which, j):
+        return remote(
+            back_out.at[which, j], back_in.at[which, j],
+            back_send.at[which, j], back_recv.at[which, j], (dp, partner),
         )
 
     def pre_copy(which, k):
@@ -165,25 +195,34 @@
 
     def z_copy(step):
         return remote(
-            z_out.at[z_peer(step)], z_in.at[step], z_send.at[step], z_recv.at[step],
-            (dp, 2 * z_peer(step) + c),
-        )
-
-    def y_copy(step):
-        return remote(
-            y_out.at[y_peer(step)], y_in.at[step], y_send.at[step], y_recv.at[step],
-            (y_peer(step) * nx + x, me),
-        )
-
-    def x_copy(step):
-        return remote(
-            x_in.at[x], x_in.at[x], x_send.at[step], x_recv.at[step], (y * nx + x_peer(step), me)
-        )
-
-    def all_copy(step):
-        return remote(
-            y_all.at[y], y_all.at[y], all_send.at[step], all_recv.at[step],
-            (y_peer(step) * nx + x, me),
+            z_out.at[z_peer(step)], z_in.at[step], z_send.at[step], z_recv.at[step], across_z(step)
+        )
+
+    def zx_copy(step):
+        return remote(
+            zx_out.at[x_peer(step)], zx_in.at[step], zx_send.at[step], zx_recv.at[step], across_x(step)
+        )
+
+    def xs_copy(step):
+        return remote(
+            xs_out.at[x_peer(step)], xs_in.at[step], xs_send.at[step], xs_recv.at[step], across_x(step)
+        )
+
+    def xz_copy(step):
+        return remote(
+            xz_out.at[z_peer(step)], xz_in.at[step], xz_send.at[step], xz_recv.at[step], across_z(step)
+        )
+
+    def y_copy(part, step, source):
+        return remote(
+            y_part.at[part, source], y_part.at[part, source],
+            y_send.at[part, step], y_recv.at[part, step], across_y(step),
+        )
+
+    def x_copy(part, step, source):
+        return remote(
+            x_part.at[part, source], x_part.at[part, source],
+            x_send.at[part, step], x_recv.at[part, step], across_x(step),
         )
 
     coef = twice((R, DV), 0)
@@ -196,6 +235,28 @@
 
     def feat(h):
         return slice(h * FD, (h + 1) * FD)
+
+    def fold_rows(source):
+        def lap(a, carry):
+            for d in range(8):
+                b = (a + d) & 15
+                row = source[0, 0, 17 + 16 * a + b].astype(f32)
+                if d:
+                    row = row + source[0, 0, 17 + 16 * b + a].astype(f32)
+                row_sum[pl.ds(pl.multiple_of((16 * d + a) * H, H), H), :] = row
+            row_sum[pl.ds(pl.multiple_of((128 + a) * H, H), H), :] = source[0, 0, 1 + a].astype(f32)
+            return carry
+
+        def last_lap(a, carry):
+            row = source[0, 0, 25 + 17 * a].astype(f32) + source[0, 0, 17 + 16 * (a + 8) + a].astype(f32)
+            row_sum[pl.ds(pl.multiple_of((144 + a) * H, H), H), :] = row
+            return carry
+
+        lax.fori_loop(0, 16, lap, 0)
+        lax.fori_loop(0, 8, last_lap, 0)
+        row_sum[152 * H : 153 * H, :] = source[0, 0, 0].astype(f32)
+
+    row_sum[153 * H :, :] = jnp.zeros(((R - 153) * H, DV), f32)
 
     def fold_norm(value):
         return sum(dot(part, fold[...], 1, 1) for part in split(value, 3))
@@ -215,17 +276,21 @@
     loads[4].wait()
     own_norm = fold_norm(kn[0, 0])
     norm_own[0] = total * coef_row + own_norm
-    pl.semaphore_wait(barrier, ns + ny + nx - 3)
-    for step in range(1, ns):
-        norm_copy(0, step).start()
+    pl.semaphore_wait(barrier, nz + ny + nx - 2)
+    mate_copy(0).start()
 
     loads[2].wait()
     loads[3].wait()
-    for h in range(H):
-        span[h] = dot(fold[...], ks[0, 0, h])
+    fold_rows(ks)
+    for h in range(H):
+        span[h] = row_sum[pl.ds(h, R, stride=H), :]
         contrib[0, h] = dot(phi_k[h], val[0, :, lanes(h)]) * coef + span[h]
     for k in range(HALF):
         other_copy(0, k).start()
+    mate_copy(0).wait_recv()
+    norm_chip[0] = norm_own[0] + norm_mate[0]
+    for step in range(1, nz):
+        norm_copy(0, step).start()
 
     causal = lax.broadcasted_iota(jnp.int32, (T, T), 0) >= lax.broadcasted_iota(jnp.int32, (T, T), 1)
     head_lane = lax.broadcasted_iota(jnp.int32, (T, H * FD), 1) // FD
@@ -241,73 +306,103 @@
         a_low[h] = a.astype(bf16)
         den[h] = jnp.broadcast_to(jnp.sum(a, axis=1, keepdims=True), (T, DV))
 
-    for step in range(1, ns):
+    def step_one(which):
+        for j in range(2):
+            k = 2 * (1 - e) + j
+            other_copy(which, k).wait_recv()
+            pair_out[which, j] = contrib[which, c * HALF + k] + other[which, k]
+            pair_copy(which, j).start()
+
+    def finish(which, k, before):
+        second = (c ^ which) == 1
+        mine = c * HALF + k
+        pre[which, mine] = before + jnp.where(second, other[which, k], 0.0)
+        pre_out[which, k] = before + jnp.where(second, 0.0, contrib[which, mine])
+        pre_copy(which, k).start()
+
+    def step_two(which):
+        first = jnp.where(which == 0, p == 0, p == pairs - 1)
+        last = jnp.where(which == 0, p == pairs - 1, p == 0)
+        for j in range(2):
+            k = 2 * e + j
+            other_copy(which, k).wait_recv()
+            pair_copy(which, j).wait_recv()
+
+            @pl.when(first)
+            def _():
+                chain_in[which, j] = jnp.zeros((R, DV), f32)
+
+            @pl.when(jnp.logical_not(first))
+            def _():
+                chain_copy(which, j).wait_recv()
+
+            before = chain_in[which, j]
+            here = contrib[which, c * HALF + k] + other[which, k]
+            there = pair_in[which, j]
+
+            @pl.when(jnp.logical_not(last))
+            def _():
+                chain_out[which, j] = before + (here + there)
+                chain_copy(which, j).start()
+
+            second = (e ^ which) == 1
+            back_out[which, j] = before + jnp.where(second, 0.0, here)
+            back_copy(which, j).start()
+            finish(which, k, before + jnp.where(second, there, 0.0))
+
+    def step_three(which):
+        for j in range(2):
+            back_copy(which, j).wait_recv()
+            finish(which, 2 * (1 - e) + j, back_in[which, j])
+
+    def step_four(which):
+        for k in range(HALF):
+            pre_copy(which, k).wait_recv()
+
+    early = 2 * p < pairs
+    late = jnp.logical_not(early)
+    step_one(0)
+
+    @pl.when(early)
+    def _():
+        step_two(0)
+
+    for step in range(1, nz):
         norm_copy(0, step).wait_recv()
-    norm = own_norm
-    for step in range(1, ns):
-        norm = norm + jnp.where(me >= step, norm_in[0, step], 0.0)
+    norm = own_norm + jnp.where(c == 1, norm_mate[0], 0.0)
+    for step in range(1, nz):
+        norm = norm + jnp.where(z >= step, norm_in[0, step], 0.0)
     norm_parts = jnp.concatenate(split(norm, 3), 0)
     two_parts = split(norm, 2)
     norm_t[...] = jnp.concatenate(two_parts + two_parts, 0).astype(f32).T.astype(bf16)
 
     loads[5].wait()
     loads[6].wait()
+    fold_rows(qs)
     part_lane = lax.broadcasted_iota(jnp.int32, (T, 3 * H), 1) & (H - 1)
     for h in range(H):
         inner = dot(phi_qt[h], norm_parts, 1, 1)
         whole = den[h] + jnp.sum(jnp.where(part_lane == h, inner, 0.0), axis=1, keepdims=True)
         den[h] = whole
         g_low[h] = (cot[0, :, lanes(h)].astype(f32) / whole).astype(bf16)
-        contrib[1, h] = dot(phi_q[h], g_low[h]) * coef + dot(fold[...], qs[0, 0, h])
+        contrib[1, h] = dot(phi_q[h], g_low[h]) * coef + row_sum[pl.ds(h, R, stride=H), :]
     for k in range(HALF):
         other_copy(1, k).start()
+    step_one(1)
     for h in range(H):
         value_part[h] = dot(a_low[h], val[0, :, lanes(h)])
 
-    ahead = jnp.clip(5 * (nz - 1 - 2 * z) // 4, -HALF, HALF)
-
-    def pass_on(which, k):
-        mine = c * HALF + k
-        first = jnp.where(which == 0, z == 0, z == nz - 1)
-        last = jnp.where(which == 0, z == nz - 1, z == 0)
-        other_copy(which, k).wait_recv()
-
-        @pl.when(first)
-        def _():
-            chain_in[which, k] = jnp.zeros((R, DV), f32)
-
-        @pl.when(jnp.logical_not(first))
-        def _():
-            chain_copy(which, k).wait_recv()
-
-        before = chain_in[which, k]
-        here = contrib[which, mine]
-        there = other[which, k]
-
-        @pl.when(jnp.logical_not(last))
-        def _():
-            chain_out[which, k] = before + (here + there)
-            chain_copy(which, k).start()
-
-        second = (c ^ which) == 1
-        pre[which, mine] = before + jnp.where(second, there, 0.0)
-        pre_out[which, k] = before + jnp.where(second, 0.0, here)
-        pre_copy(which, k).start()
-
-    def chain_step(i, carry):
-        for which, lag in ((0, jnp.maximum(-ahead, 0)), (1, jnp.maximum(ahead, 0))):
-            k = i - lag
-
-            @pl.when((k >= 0) & (k < HALF))
-            def _():
-                pass_on(which, k)
-
-        return carry
-
-    lax.fori_loop(0, 2 * HALF, chain_step, 0)
-    for which in range(2):
-        for k in range(HALF):
-            pre_copy(which, k).wait_recv()
+    @pl.when(late)
+    def _():
+        def either(i, carry):
+            step_two(i ^ (p == pairs - 1).astype(jnp.int32))
+            return carry
+
+        lax.fori_loop(0, 2, either, 0)
+        step_three(1)
+
+    step_three(0)
+    step_four(0)
 
     lane = lax.broadcasted_iota(jnp.int32, (T, DV), 1)
     gden_all = jnp.zeros((T, DV), f32)
@@ -328,7 +423,10 @@
         total = jnp.where(head_row == h, every, total)
     loads[7].wait()
     norm_own[1] = total * coef_row + fold_norm(qn[0, 0])
-    for step in range(1, ns):
+    mate_copy(1).start()
+    mate_copy(1).wait_recv()
+    norm_chip[1] = norm_own[1] + norm_mate[1]
+    for step in range(1, nz):
         norm_copy(1, step).start()
 
     high, low = split(gden_t[...], 2)
@@ -339,17 +437,24 @@
         up = dot(p_low[h], g_low[h], 1, 1) + dot(norm_t[...], only)
         u = qt[feat(h), :]
         dproj_t[feat(h), :] = feature_grad(u, up) + dot(kt[feat(h), :].astype(bf16), gs[h], 1, 1)
+
+    @pl.when(early)
+    def _():
+        step_two(1)
+        step_three(1)
+
+    step_four(1)
     for h in range(H):
         p_low[h] = pre[1, h].astype(bf16)
         vg[0, :, lanes(h)] = (dot(a_low[h], g_low[h], 0, 0) + dot(phi_kt[h], p_low[h])).astype(bf16)
     store_vg = pltpu.make_async_copy(vg, vg_h, out_sem.at[0])
     store_vg.start()
 
-    for step in range(1, ns):
+    for step in range(1, nz):
         norm_copy(1, step).wait_recv()
-    norm = jnp.zeros((H, R), f32)
-    for step in range(1, ns):
-        norm = norm + jnp.where(me + (ns - step) < ns, norm_in[1, step], 0.0)
+    norm = jnp.where(c == 0, norm_mate[1], 0.0)
+    for step in range(1, nz):
+        norm = norm + jnp.where(z < step, norm_in[1, step], 0.0)
     parts = split(norm, 3)
     norm_t[...] = jnp.concatenate(parts + [jnp.zeros_like(parts[0])], 0).astype(f32).T.astype(bf16)
     for h in range(H):
@@ -369,8 +474,12 @@
         term[2 * k + c] = dot(tok[0, :, chunk], dproj, 0, 0)
     for k in range(nz):
         core_copy(k).wait_recv()
-    for k in range(nz):
-        z_out[k] = term[2 * k + c] + core_in[k]
+        both = term[2 * k + c] + core_in[k]
+        z_out[k] = both[:half]
+        for j in range(nx):
+            xs_out[j, k] = both[half + j * piece : half + (j + 1) * piece]
+    for step in range(1, nx):
+        xs_copy(step).start()
     for step in range(1, nz):
         z_copy(step).start()
 
@@ -380,63 +489,82 @@
     store_tg = pltpu.make_async_copy(tg, tg_h, out_sem.at[1])
     store_tg.start()
 
+    for step in range(1, nx):
+        xs_copy(step).wait_recv()
+    for k in range(nz):
+        acc = xs_out[x, k]
+        for step in range(1, nx):
+            acc = acc + xs_in[step, k]
+        xz_out[k] = acc
+    for step in range(1, nz):
+        xz_copy(step).start()
     acc = z_out[z]
     for step in range(1, nz):
         z_copy(step).wait_recv()
         acc = acc + z_in[step]
-    y_out[...] = acc.reshape(ny, piece, 2 * H * FD)
+    for j in range(nx):
+        zx_out[j] = acc[j * piece : (j + 1) * piece]
+    for step in range(1, nx):
+        zx_copy(step).start()
+    acc = xz_out[z]
+    for step in range(1, nz):
+        xz_copy(step).wait_recv()
+        acc = acc + xz_in[step]
+    y_part[1, y] = acc
     for step in range(1, ny):
-        y_copy(step).start()
-    acc = y_out[y]
+        y_copy(1, step, y).start()
+    acc = zx_out[x]
+    for step in range(1, nx):
+        zx_copy(step).wait_recv()
+        acc = acc + zx_in[step]
+    y_part[0, y] = acc
     for step in range(1, ny):
-        y_copy(step).wait_recv()
-        acc = acc + y_in[step]
-    x_in[x] = acc
-    for step in range(1, nx):
-        x_copy(step).start()
-    for step in range(1, nx):
-        source = lax.rem(x + nx - step, nx)
-        remote(
-            x_in.at[source], x_in.at[source], x_send.at[step], x_recv.at[step],
-            (y * nx + x_peer(step), me),
-        ).wait_recv()
-    acc = x_in[0]
-    for j in range(1, nx):
-        acc = acc + x_in[j]
-    y_all[y] = acc * (1.0 / (ny * nx))
-    for step in range(1, ny):
-        all_copy(step).start()
-    for step in range(1, ny):
-        source = lax.rem(y + ny - step, ny)
-        remote(
-            y_all.at[source], y_all.at[source], all_send.at[step], all_recv.at[step],
-            (y_peer(step) * nx + x, me),
-        ).wait_recv()
-    wg[...] = y_all[...].reshape(rows, 2 * H * FD)
+        y_copy(0, step, y).start()
+    for part in (1, 0):
+        for step in range(1, ny):
+            y_copy(part, step, lax.rem(y + ny - step, ny)).wait_recv()
+        acc = y_part[part, 0]
+        for j in range(1, ny):
+            acc = acc + y_part[part, j]
+        x_part[part, x] = acc * (1.0 / (ny * nx))
+        for step in range(1, nx):
+            x_copy(part, step, x).start()
+    for part in (1, 0):
+        for step in range(1, nx):
+            x_copy(part, step, lax.rem(x + nx - step, nx)).wait_recv()
+    wg[...] = x_part[...].reshape(rows, 2 * H * FD)
     store_wg = pltpu.make_async_copy(wg, wg_h, out_sem.at[2])
     store_wg.start()
 
     for which in range(2):
-        for step in range(1, ns):
+        mate_copy(which).wait_send()
+        for step in range(1, nz):
             norm_copy(which, step).wait_send()
-        last = (z == nz - 1) if which == 0 else (z == 0)
+        last = (p == pairs - 1) if which == 0 else (p == 0)
         for k in range(HALF):
             other_copy(which, k).wait_send()
             pre_copy(which, k).wait_send()
+        for j in range(2):
+            pair_copy(which, j).wait_send()
+            back_copy(which, j).wait_send()
 
             @pl.when(jnp.logical_not(last))
             def _():
-                chain_copy(which, k).wait_send()
+                chain_copy(which, j).wait_send()
 
     for k in range(nz):
         core_copy(k).wait_send()
     for step in range(1, nz):
         z_copy(step).wait_send()
-    for step in range(1, ny):
-        y_copy(step).wait_send()
-        all_copy(step).wait_send()
+        xz_copy(step).wait_send()
     for step in range(1, nx):
-        x_copy(step).wait_send()
+        xs_copy(step).wait_send()
+        zx_copy(step).wait_send()
+    for part in range(2):
+        for step in range(1, ny):
+            y_copy(part, step, y).wait_send()
+        for step in range(1, nx):
+            x_copy(part, step, x).wait_send()
     store_vg.wait()
     store_tg.wait()
     store_wg.wait()
@@ -446,8 +574,10 @@
     ns, ny, nx, d_model = sizes
     nz = ns // 2
     rows = d_model // ns
-    piece = rows // ny
+    half = rows // 2
+    piece = half // nx
     width = 2 * H * FD
+    key_span, query_span = (jnp.swapaxes(a, 2, 3) for a in (key_span, query_span))
     args = (tokens, qk_weight, values, cotangent, key_span, key_norm, query_span, query_norm)
     out_shape = (
         jax.ShapeDtypeStruct((1, T, d_model), bf16),
@@ -475,32 +605,48 @@
         vmem((H, R, DV), f32),
         vmem((2, H, R, DV), f32),
         vmem((2, HALF, R, DV), f32),
-        vmem((2, HALF, R, DV), f32),
-        vmem((2, HALF, R, DV), f32),
+        vmem((2, 2, R, DV), f32),
+        vmem((2, 2, R, DV), f32),
+        vmem((2, 2, R, DV), f32),
+        vmem((2, 2, R, DV), f32),
+        vmem((2, 2, R, DV), f32),
+        vmem((2, 2, R, DV), f32),
         vmem((2, H, R, DV), f32),
         vmem((2, HALF, R, DV), f32),
+        vmem((R * H, DV), f32),
         vmem((2, H, R), f32),
-        vmem((2, ns, H, R), f32),
+        vmem((2, H, R), f32),
+        vmem((2, H, R), f32),
+        vmem((2, nz, H, R), f32),
         vmem((H, T), f32),
         vmem((width, T), f32),
         vmem((ns, rows, width), f32),
         vmem((nz, rows, width), f32),
-        vmem((nz, rows, width), f32),
-        vmem((nz, rows, width), f32),
-        vmem((ny, piece, width), f32),
-        vmem((ny, piece, width), f32),
+        vmem((nz, half, width), f32),
+        vmem((nz, half, width), f32),
         vmem((nx, piece, width), f32),
-        vmem((ny, piece, width), f32),
+        vmem((nx, piece, width), f32),
+        vmem((nx, nz, piece, width), f32),
+        vmem((nx, nz, piece, width), f32),
+        vmem((nz, piece, width), f32),
+        vmem((nz, piece, width), f32),
+        vmem((2, ny, piece, width), f32),
+        vmem((2, nx, piece, width), f32),
         dma((8,)), dma((3,)),
-        dma((2, ns)), dma((2, ns)),
+        dma((2,)), dma((2,)),
+        dma((2, nz)), dma((2, nz)),
         dma((2, HALF)), dma((2, HALF)),
-        dma((2, HALF)), dma((2, HALF)),
+        dma((2, 2)), dma((2, 2)),
+        dma((2, 2)), dma((2, 2)),
+        dma((2, 2)), dma((2, 2)),
         dma((2, HALF)), dma((2, HALF)),
         dma((nz,)), dma((nz,)),
         dma((nz,)), dma((nz,)),
-        dma((ny,)), dma((ny,)),
         dma((nx,)), dma((nx,)),
-        dma((ny,)), dma((ny,)),
+        dma((nx,)), dma((nx,)),
+        dma((nz,)), dma((nz,)),
+        dma((2, ny)), dma((2, ny)),
+        dma((2, nx)), dma((2, nx)),
     ]
     return pl.pallas_call(
         functools.partial(kernel, sizes),

time: 115 us -> 99.5 us (0.87)
  the two profiles are of different devices: /device:TPU:16 before, /device:TPU:1 now
where the time goes in v2:
time: 99.5 us; the launch traced here: 99 us
  Pallas kernels  88.5 us (89%)
  local copies, waits for them, and re-layouts  9.83 us (10%)
    pallas_call x1, Pallas kernels, on_device(): pl.pallas_call(functools.partial(kernel, sizes), out_shape=out_shape, in_...  88.5 us
    unnamed x19, local copies, waits for them, and re-layouts  9.83 us

profile of v2, /device:TPU:1, one launch (start us, length us, event | category | flops | bytes accessed | tf_op | source)
XLA Modules:
  0.0 99.0 jit_solution(17918116357217829161)
XLA Ops:
  0.6 0.0 copy-start
  0.6 1.2 %copy-done = bf16[2048,256]{1,0:T(8,128)(2,1)S(1)} copy-done((bf16[2048,256]{1,0:T(8,128)(2,1)S(1)}, bf16[2048,256]{1,0:T(8,128)(2,1)}, u32[]{:S(2)}) %copy-start) | copy-done | bytes 1048600
  1.9 0.0 copy-start.1
  1.9 1.1 %copy-done.1 = bf16[1,1,8,273,128]{4,2,3,1,0:T(8,128)(2,1)S(1)} copy-done((bf16[1,1,8,273,128]{4,2,3,1,0:T(8,128)(2,1)S(1)}, bf16[1,1,8,273,128]{4,2,3,1,0:T(8,128)(2,1)}, u32[]{:S(2)}) %copy-start.1) | copy-done | bytes 559128
  2.9 0.0 copy-start.2
  2.9 1.1 %copy-done.2 = bf16[1,1,8,273,128]{4,2,3,1,0:T(8,128)(2,1)S(1)} copy-done((bf16[1,1,8,273,128]{4,2,3,1,0:T(8,128)(2,1)S(1)}, bf16[1,1,8,273,128]{4,2,3,1,0:T(8,128)(2,1)}, u32[]{:S(2)}) %copy-start.2) | copy-done | bytes 559128
  4.0 0.0 copy-start.3
  4.0 1.0 %copy-done.3 = bf16[1,128,2048]{2,1,0:T(8,128)(2,1)S(1)} copy-done((bf16[1,128,2048]{2,1,0:T(8,128)(2,1)S(1)}, bf16[1,128,2048]{2,1,0:T(8,128)(2,1)}, u32[]{:S(2)}) %copy-start.3) | copy-done | bytes 524312
  5.0 0.0 copy-start.4
  5.0 0.9 copy-done.4
  6.0 0.0 copy-start.5
  6.0 0.9 copy-done.5
  6.9 0.0 copy-start.6
  6.9 0.7 copy-done.6
  7.6 0.0 copy-start.7
  7.6 0.7 copy-done.7
  8.3 88.5 %shard_map.103 = (bf16[1,128,2048]{2,1,0:T(8,128)(2,1)S(1)}, bf16[1,128,1024]{2,1,0:T(8,128)(2,1)S(1)}, f32[128,256]{1,0:T(8,128)S(1)}) custom-call(bf16[1,128,2048]{2,1,0:T(8,128)(2,1)S(1)} %copy-done.3, bf16[2048,256]{1,0:T(8,128)(2,1)S(1)} %copy-done, bf16[1,128,1024]{2,1,0:T(8,128)(2,1)S(1)} %copy-done.4, bf16[1,128,1024]{2,1,0:T(8,128)(2,1)S(1)} %copy-done.5, ...), custom_call_target="tpu_custom_call" | custom-call | tf_op jit(solution)/shard_map/pallas_call | solution.py:651
  96.8 0.8 copy.14
  97.6 0.7 copy.15
  98.3 0.7 copy.16
Async XLA Ops:
  0.6 1.2 %copy-start = (bf16[2048,256]{1,0:T(8,128)(2,1)S(1)}, bf16[2048,256]{1,0:T(8,128)(2,1)}, u32[]{:S(2)}) copy-start(bf16[2048,256]{1,0:T(8,128)(2,1)} %w_h.1) | copy-start | bytes 3145732
  1.9 1.1 %copy-start.1 = (bf16[1,1,8,273,128]{4,2,3,1,0:T(8,128)(2,1)S(1)}, bf16[1,1,8,273,128]{4,2,3,1,0:T(8,128)(2,1)}, u32[]{:S(2)}) copy-start(bf16[1,1,8,273,128]{4,2,3,1,0:T(8,128)(2,1)} %param.12) | copy-start | bytes 1677316
  2.9 1.1 %copy-start.2 = (bf16[1,1,8,273,128]{4,2,3,1,0:T(8,128)(2,1)S(1)}, bf16[1,1,8,273,128]{4,2,3,1,0:T(8,128)(2,1)}, u32[]{:S(2)}) copy-start(bf16[1,1,8,273,128]{4,2,3,1,0:T(8,128)(2,1)} %param.14) | copy-start | bytes 1677316
  4.0 1.0 %copy-start.3 = (bf16[1,128,2048]{2,1,0:T(8,128)(2,1)S(1)}, bf16[1,128,2048]{2,1,0:T(8,128)(2,1)}, u32[]{:S(2)}) copy-start(bf16[1,128,2048]{2,1,0:T(8,128)(2,1)} %tok_h.1) | copy-start | bytes 1572868
  5.0 0.9 copy-start.4
  6.0 0.9 copy-start.5
  6.9 0.7 copy-start.6
  7.6 0.7 copy-start.7

commit v3 on v2

--- a/solution.py
+++ b/solution.py
@@ -83,19 +83,19 @@
     qt, kt, phi_q, phi_k, phi_qt, phi_kt, fold,
     score, a_low, value_part, den, g_low, gs, p_low, norm_t,
     span, contrib, other, pair_out, pair_in, chain_in, chain_out, back_out, back_in, pre, pre_out,
-    row_sum, norm_own, norm_mate, norm_chip, norm_in, gden_t, dproj_t,
-    term, core_in, z_out, z_in, zx_out, zx_in, xs_out, xs_in, xz_out, xz_in, y_part, x_part,
+    row_sum, query_sum, norm_own, norm_mate, norm_chip, norm_in, gden_t, dproj_t,
+    term, core_in, xs_out, xs_in, xz_out, xz_in, y_part, x_part,
     in_sem, out_sem,
     mate_send, mate_recv, norm_send, norm_recv, other_send, other_recv, pair_send, pair_recv,
     chain_send, chain_recv, back_send, back_recv, pre_send, pre_recv,
-    core_send, core_recv, z_send, z_recv, zx_send, zx_recv, xs_send, xs_recv, xz_send, xz_recv,
+    core_send, core_recv, xs_send, xs_recv, xz_send, xz_recv,
     y_send, y_recv, x_send, x_recv,
 ):
     ns, ny, nx, d_model = sizes
     nz = ns // 2
     rows = d_model // ns
     pairs = nz // 2
-    half = rows // 2
+    half = H * FD
     piece = half // nx
     dp = lax.axis_index("dp")
     me = lax.axis_index("seq")
@@ -188,29 +188,22 @@
             pre_send.at[which, k], pre_recv.at[which, k], (dp, mate),
         )
 
-    def core_copy(k):
-        return remote(
-            term.at[2 * k + (1 - c)], core_in.at[k], core_send.at[k], core_recv.at[k], (dp, mate)
-        )
-
-    def z_copy(step):
-        return remote(
-            z_out.at[z_peer(step)], z_in.at[step], z_send.at[step], z_recv.at[step], across_z(step)
-        )
-
-    def zx_copy(step):
-        return remote(
-            zx_out.at[x_peer(step)], zx_in.at[step], zx_send.at[step], zx_recv.at[step], across_x(step)
-        )
-
-    def xs_copy(step):
-        return remote(
-            xs_out.at[x_peer(step)], xs_in.at[step], xs_send.at[step], xs_recv.at[step], across_x(step)
-        )
-
-    def xz_copy(step):
-        return remote(
-            xz_out.at[z_peer(step)], xz_in.at[step], xz_send.at[step], xz_recv.at[step], across_z(step)
+    def core_copy(part, k):
+        return remote(
+            term.at[part, 2 * k + (1 - c)], core_in.at[part, k],
+            core_send.at[part, k], core_recv.at[part, k], (dp, mate),
+        )
+
+    def xs_copy(part, step):
+        return remote(
+            xs_out.at[part, x_peer(step)], xs_in.at[part, step],
+            xs_send.at[part, step], xs_recv.at[part, step], across_x(step),
+        )
+
+    def xz_copy(part, step):
+        return remote(
+            xz_out.at[part, z_peer(step)], xz_in.at[part, step],
+            xz_send.at[part, step], xz_recv.at[part, step], across_z(step),
         )
 
     def y_copy(part, step, source):
@@ -236,7 +229,7 @@
     def feat(h):
         return slice(h * FD, (h + 1) * FD)
 
-    def fold_rows(source):
+    def fold_rows(source, row_sum):
         def lap(a, carry):
             for d in range(8):
                 b = (a + d) & 15
@@ -255,8 +248,7 @@
         lax.fori_loop(0, 16, lap, 0)
         lax.fori_loop(0, 8, last_lap, 0)
         row_sum[152 * H : 153 * H, :] = source[0, 0, 0].astype(f32)
-
-    row_sum[153 * H :, :] = jnp.zeros(((R - 153) * H, DV), f32)
+        row_sum[153 * H :, :] = jnp.zeros(((R - 153) * H, DV), f32)
 
     def fold_norm(value):
         return sum(dot(part, fold[...], 1, 1) for part in split(value, 3))
@@ -271,7 +263,6 @@
     for h in range(H):
         phi = features(kt[feat(h), :])
         phi_k[h] = phi.astype(bf16)
-        phi_kt[h] = phi.T.astype(bf16)
         total = jnp.where(head_row == h, dot(ones, phi_k[h], 1, 1), total)
     loads[4].wait()
     own_norm = fold_norm(kn[0, 0])
@@ -281,7 +272,7 @@
 
     loads[2].wait()
     loads[3].wait()
-    fold_rows(ks)
+    fold_rows(ks, row_sum)
     for h in range(H):
         span[h] = row_sum[pl.ds(h, R, stride=H), :]
         contrib[0, h] = dot(phi_k[h], val[0, :, lanes(h)]) * coef + span[h]
@@ -362,6 +353,8 @@
     early = 2 * p < pairs
     late = jnp.logical_not(early)
     step_one(0)
+    loads[6].wait()
+    fold_rows(qs, query_sum)
 
     @pl.when(early)
     def _():
@@ -377,20 +370,19 @@
     norm_t[...] = jnp.concatenate(two_parts + two_parts, 0).astype(f32).T.astype(bf16)
 
     loads[5].wait()
-    loads[6].wait()
-    fold_rows(qs)
     part_lane = lax.broadcasted_iota(jnp.int32, (T, 3 * H), 1) & (H - 1)
     for h in range(H):
         inner = dot(phi_qt[h], norm_parts, 1, 1)
         whole = den[h] + jnp.sum(jnp.where(part_lane == h, inner, 0.0), axis=1, keepdims=True)
         den[h] = whole
         g_low[h] = (cot[0, :, lanes(h)].astype(f32) / whole).astype(bf16)
-        contrib[1, h] = dot(phi_q[h], g_low[h]) * coef + row_sum[pl.ds(h, R, stride=H), :]
+        contrib[1, h] = dot(phi_q[h], g_low[h]) * coef + query_sum[pl.ds(h, R, stride=H), :]
     for k in range(HALF):
         other_copy(1, k).start()
     step_one(1)
     for h in range(H):
         value_part[h] = dot(a_low[h], val[0, :, lanes(h)])
+        phi_kt[h] = phi_k[h].astype(f32).T.astype(bf16)
 
     @pl.when(late)
     def _():
@@ -404,6 +396,60 @@
     step_three(0)
     step_four(0)
 
+    def send_terms(part):
+        left = dproj_t[part * half : (part + 1) * half, :].astype(bf16)
+        for k in range(nz):
+            chunk = pl.ds(pl.multiple_of((2 * k + 1 - c) * rows, rows), rows)
+            term[part, 2 * k + 1 - c] = dot(left, tok[0, :, chunk])
+            core_copy(part, k).start()
+        for k in range(nz):
+            chunk = pl.ds(pl.multiple_of((2 * k + c) * rows, rows), rows)
+            term[part, 2 * k + c] = dot(left, tok[0, :, chunk])
+
+    def send_x(part):
+        for k in range(nz):
+            core_copy(part, k).wait_recv()
+            both = term[part, 2 * k + c] + core_in[part, k]
+            for j in range(nx):
+                xs_out[part, j, k] = both[j * piece : (j + 1) * piece]
+        for step in range(1, nx):
+            xs_copy(part, step).start()
+
+    def send_z(part):
+        for step in range(1, nx):
+            xs_copy(part, step).wait_recv()
+        for k in range(nz):
+            acc = xs_out[part, x, k]
+            for step in range(1, nx):
+                acc = acc + xs_in[part, step, k]
+            xz_out[part, k] = acc
+        for step in range(1, nz):
+            xz_copy(part, step).start()
+
+    def send_y(part):
+        acc = xz_out[part, z]
+        for step in range(1, nz):
+            xz_copy(part, step).wait_recv()
+            acc = acc + xz_in[part, step]
+        y_part[part, y] = acc
+        for step in range(1, ny):
+            y_copy(part, step, y).start()
+
+    def send_all(part):
+        for step in range(1, ny):
+            y_copy(part, step, lax.rem(y + ny - step, ny)).wait_recv()
+        acc = y_part[part, 0]
+        for j in range(1, ny):
+            acc = acc + y_part[part, j]
+        x_part[part, x] = acc * (1.0 / (ny * nx))
+        for step in range(1, nx):
+            x_copy(part, step, x).start()
+
+    def collect(part):
+        for step in range(1, nx):
+            x_copy(part, step, lax.rem(x + nx - step, nx)).wait_recv()
+        wg[:, part * half : (part + 1) * half] = x_part[part].reshape(half, rows).T
+
     lane = lax.broadcasted_iota(jnp.int32, (T, DV), 1)
     gden_all = jnp.zeros((T, DV), f32)
     for h in range(H):
@@ -412,8 +458,7 @@
         weighted = jnp.sum(cot[0, :, lanes(h)].astype(f32) * numer, axis=1, keepdims=True)
         gden = -weighted / (den[h] * den[h])
         gden_all = jnp.where(lane == h, gden, gden_all)
-        ga = jnp.where(causal, dot(g_low[h], val[0, :, lanes(h)], 1, 1) + gden, 0.0)
-        gs[h] = (ga * (1.0 + score[h]) * (1.0 / math.sqrt(FD))).astype(bf16)
+        den[h] = jnp.broadcast_to(gden, (T, DV))
     gden_t[...] = gden_all.T[:H]
     gden_parts = jnp.concatenate(split(gden_t[...], 3), 0)
     total = jnp.zeros((H, R), f32)
@@ -433,10 +478,14 @@
     gden_rows = jnp.concatenate([high, high, low, low], 0)
     four_row = lax.broadcasted_iota(jnp.int32, (4 * H, T), 0) & (H - 1)
     for h in range(H):
+        ga = jnp.where(causal, dot(g_low[h], val[0, :, lanes(h)], 1, 1) + den[h], 0.0)
+        gs[h] = (ga * (1.0 + score[h]) * (1.0 / math.sqrt(FD))).astype(bf16)
         only = jnp.where(four_row == h, gden_rows, jnp.zeros_like(gden_rows))
         up = dot(p_low[h], g_low[h], 1, 1) + dot(norm_t[...], only)
         u = qt[feat(h), :]
         dproj_t[feat(h), :] = feature_grad(u, up) + dot(kt[feat(h), :].astype(bf16), gs[h], 1, 1)
+    send_terms(0)
+    send_x(0)
 
     @pl.when(early)
     def _():
@@ -444,12 +493,6 @@
         step_three(1)
 
     step_four(1)
-    for h in range(H):
-        p_low[h] = pre[1, h].astype(bf16)
-        vg[0, :, lanes(h)] = (dot(a_low[h], g_low[h], 0, 0) + dot(phi_kt[h], p_low[h])).astype(bf16)
-    store_vg = pltpu.make_async_copy(vg, vg_h, out_sem.at[0])
-    store_vg.start()
-
     for step in range(1, nz):
         norm_copy(1, step).wait_recv()
     norm = jnp.where(c == 0, norm_mate[1], 0.0)
@@ -459,80 +502,33 @@
     norm_t[...] = jnp.concatenate(parts + [jnp.zeros_like(parts[0])], 0).astype(f32).T.astype(bf16)
     for h in range(H):
         only = jnp.where(four_row == h, 1.0, 0.0).astype(bf16)
+        p_low[h] = pre[1, h].astype(bf16)
         up = dot(p_low[h], val[0, :, lanes(h)], 1, 1) + dot(norm_t[...], only)
         u = kt[feat(h), :]
         inner = dot(qt[feat(h), :].astype(bf16), gs[h])
         dproj_t[H * FD + h * FD : H * FD + (h + 1) * FD, :] = feature_grad(u, up) + inner
+    send_terms(1)
+    send_z(0)
+    send_x(1)
+
+    for h in range(H):
+        vg[0, :, lanes(h)] = (dot(a_low[h], g_low[h], 0, 0) + dot(phi_kt[h], p_low[h])).astype(bf16)
+    store_vg = pltpu.make_async_copy(vg, vg_h, out_sem.at[0])
+    store_vg.start()
     dproj = dproj_t[...].T.astype(bf16)
-
-    for k in range(nz):
-        chunk = pl.ds(pl.multiple_of((2 * k + 1 - c) * rows, rows), rows)
-        term[2 * k + 1 - c] = dot(tok[0, :, chunk], dproj, 0, 0)
-        core_copy(k).start()
-    for k in range(nz):
-        chunk = pl.ds(pl.multiple_of((2 * k + c) * rows, rows), rows)
-        term[2 * k + c] = dot(tok[0, :, chunk], dproj, 0, 0)
-    for k in range(nz):
-        core_copy(k).wait_recv()
-        both = term[2 * k + c] + core_in[k]
-        z_out[k] = both[:half]
-        for j in range(nx):
-            xs_out[j, k] = both[half + j * piece : half + (j + 1) * piece]
-    for step in range(1, nx):
-        xs_copy(step).start()
-    for step in range(1, nz):
-        z_copy(step).start()
-
     cols = min(512, d_model)
     for j in range(d_model // cols):
         tg[0, :, j * cols : (j + 1) * cols] = dot(dproj, w[j * cols : (j + 1) * cols, :], 1, 1).astype(bf16)
     store_tg = pltpu.make_async_copy(tg, tg_h, out_sem.at[1])
     store_tg.start()
 
-    for step in range(1, nx):
-        xs_copy(step).wait_recv()
-    for k in range(nz):
-        acc = xs_out[x, k]
-        for step in range(1, nx):
-            acc = acc + xs_in[step, k]
-        xz_out[k] = acc
-    for step in range(1, nz):
-        xz_copy(step).start()
-    acc = z_out[z]
-    for step in range(1, nz):
-        z_copy(step).wait_recv()
-        acc = acc + z_in[step]
-    for j in range(nx):
-        zx_out[j] = acc[j * piece : (j + 1) * piece]
-    for step in range(1, nx):
-        zx_copy(step).start()
-    acc = xz_out[z]
-    for step in range(1, nz):
-        xz_copy(step).wait_recv()
-        acc = acc + xz_in[step]
-    y_part[1, y] = acc
-    for step in range(1, ny):
-        y_copy(1, step, y).start()
-    acc = zx_out[x]
-    for step in range(1, nx):
-        zx_copy(step).wait_recv()
-        acc = acc + zx_in[step]
-    y_part[0, y] = acc
-    for step in range(1, ny):
-        y_copy(0, step, y).start()
-    for part in (1, 0):
-        for step in range(1, ny):
-            y_copy(part, step, lax.rem(y + ny - step, ny)).wait_recv()
-        acc = y_part[part, 0]
-        for j in range(1, ny):
-            acc = acc + y_part[part, j]
-        x_part[part, x] = acc * (1.0 / (ny * nx))
-        for step in range(1, nx):
-            x_copy(part, step, x).start()
-    for part in (1, 0):
-        for step in range(1, nx):
-            x_copy(part, step, lax.rem(x + nx - step, nx)).wait_recv()
-    wg[...] = x_part[...].reshape(rows, 2 * H * FD)
+    send_y(0)
+    send_z(1)
+    send_all(0)
+    send_y(1)
+    collect(0)
+    send_all(1)
+    collect(1)
     store_wg = pltpu.make_async_copy(wg, wg_h, out_sem.at[2])
     store_wg.start()
 
@@ -552,18 +548,15 @@
             def _():
                 chain_copy(which, j).wait_send()
 
-    for k in range(nz):
-        core_copy(k).wait_send()
-    for step in range(1, nz):
-        z_copy(step).wait_send()
-        xz_copy(step).wait_send()
-    for step in range(1, nx):
-        xs_copy(step).wait_send()
-        zx_copy(step).wait_send()
     for part in range(2):
+        for k in range(nz):
+            core_copy(part, k).wait_send()
+        for step in range(1, nz):
+            xz_copy(part, step).wait_send()
         for step in range(1, ny):
             y_copy(part, step, y).wait_send()
         for step in range(1, nx):
+            xs_copy(part, step).wait_send()
             x_copy(part, step, x).wait_send()
     store_vg.wait()
     store_tg.wait()
@@ -574,7 +567,7 @@
     ns, ny, nx, d_model = sizes
     nz = ns // 2
     rows = d_model // ns
-    half = rows // 2
+    half = H * FD
     piece = half // nx
     width = 2 * H * FD
     key_span, query_span = (jnp.swapaxes(a, 2, 3) for a in (key_span, query_span))
@@ -614,24 +607,21 @@
         vmem((2, H, R, DV), f32),
         vmem((2, HALF, R, DV), f32),
         vmem((R * H, DV), f32),
+        vmem((R * H, DV), f32),
         vmem((2, H, R), f32),
         vmem((2, H, R), f32),
         vmem((2, H, R), f32),
         vmem((2, nz, H, R), f32),
         vmem((H, T), f32),
         vmem((width, T), f32),
-        vmem((ns, rows, width), f32),
-        vmem((nz, rows, width), f32),
-        vmem((nz, half, width), f32),
-        vmem((nz, half, width), f32),
-        vmem((nx, piece, width), f32),
-        vmem((nx, piece, width), f32),
-        vmem((nx, nz, piece, width), f32),
-        vmem((nx, nz, piece, width), f32),
-        vmem((nz, piece, width), f32),
-        vmem((nz, piece, width), f32),
-        vmem((2, ny, piece, width), f32),
-        vmem((2, nx, piece, width), f32),
+        vmem((2, ns, half, rows), f32),
+        vmem((2, nz, half, rows), f32),
+        vmem((2, nx, nz, piece, rows), f32),
+        vmem((2, nx, nz, piece, rows), f32),
+        vmem((2, nz, piece, rows), f32),
+        vmem((2, nz, piece, rows), f32),
+        vmem((2, ny, piece, rows), f32),
+        vmem((2, nx, piece, rows), f32),
         dma((8,)), dma((3,)),
         dma((2,)), dma((2,)),
         dma((2, nz)), dma((2, nz)),
@@ -640,11 +630,9 @@
         dma((2, 2)), dma((2, 2)),
         dma((2, 2)), dma((2, 2)),
         dma((2, HALF)), dma((2, HALF)),
-        dma((nz,)), dma((nz,)),
-        dma((nz,)), dma((nz,)),
-        dma((nx,)), dma((nx,)),
-        dma((nx,)), dma((nx,)),
-        dma((nz,)), dma((nz,)),
+        dma((2, nz)), dma((2, nz)),
+        dma((2, nx)), dma((2, nx)),
+        dma((2, nz)), dma((2, nz)),
         dma((2, ny)), dma((2, ny)),
         dma((2, nx)), dma((2, nx)),
     ]
@@ -655,7 +643,7 @@
         out_specs=(pl.BlockSpec(memory_space=pl.ANY),) * 3,
         scratch_shapes=scratch,
         compiler_params=pltpu.CompilerParams(
-            collective_id=0, has_side_effects=True, vmem_limit_bytes=48 * 1024 * 1024
+            collective_id=0, has_side_effects=True, vmem_limit_bytes=60 * 1024 * 1024
         ),
     )(*args)
 

time: 99.5 us -> 90.2 us (0.907)
  local copies, waits for them, and re-layouts: 9.83 us -> 3.58 us
  Pallas kernels: 88.5 us -> 85.3 us
    unnamed x19 -> x7, local copies, waits for them, and re-layouts: 9.83 us -> 3.58 us
    pallas_call x1, Pallas kernels: 88.5 us -> 85.3 us  [on_device(): pl.pallas_call(functools.partial(kernel, sizes), out_shape=out_shape, in_...]
where the time goes in v3:
time: 90.2 us; the launch traced here: 89.5 us
  Pallas kernels  85.3 us (95%)
  local copies, waits for them, and re-layouts  3.58 us (4%)
    pallas_call x1, Pallas kernels, on_device(): pl.pallas_call(functools.partial(kernel, sizes), out_shape=out_shape, in_...  85.3 us
    unnamed x7, local copies, waits for them, and re-layouts  3.58 us

profile of v3, /device:TPU:1, one launch (start us, length us, event | category | flops | bytes accessed | tf_op | source)
XLA Modules:
  0.0 89.5 jit_solution(3836030189077668853)
XLA Ops:
  0.6 85.3 %shard_map.103 = (bf16[1,128,2048]{2,1,0:T(8,128)(2,1)}, bf16[1,128,1024]{2,1,0:T(8,128)(2,1)}, f32[128,256]{1,0:T(8,128)}) custom-call(bf16[1,128,2048]{2,1,0:T(8,128)(2,1)} %tok_h.1, bf16[2048,256]{1,0:T(8,128)(2,1)} %w_h.1, bf16[1,128,1024]{2,1,0:T(8,128)(2,1)} %val_h.1, bf16[1,128,1024]{2,1,0:T(8,128)(2,1)} %cot_h.1, ...), custom_call_target="tpu_custom_call" | custom-call | tf_op jit(solution)/shard_map/pallas_call | solution.py:639
  85.9 0.0 copy-start
  85.9 1.9 %copy.14 = bf16[1,128,2048]{2,1,0:T(8,128)(2,1)} copy(bf16[1,128,2048]{2,1,0:T(8,128)(2,1)} %get-tuple-element.6) | data formatting | bytes 1048576
  87.8 0.0 copy-done
  87.8 0.0 copy-start.1
  87.8 0.7 copy.15
  88.5 0.3 copy-done.1
  88.8 0.7 copy.16
Async XLA Ops:
  85.9 1.9 %copy-start = (bf16[1,128,1024]{2,1,0:T(8,128)(2,1)S(1)}, bf16[1,128,1024]{2,1,0:T(8,128)(2,1)}, u32[]{:S(2)}) copy-start(bf16[1,128,1024]{2,1,0:T(8,128)(2,1)} %get-tuple-element.7) | copy-start | bytes 786436
  87.8 1.0 %copy-start.1 = (f32[128,256]{1,0:T(8,128)S(1)}, f32[128,256]{1,0:T(8,128)}, u32[]{:S(2)}) copy-start(f32[128,256]{1,0:T(8,128)} %get-tuple-element.8) | copy-start | bytes 393220

commit v4 on v3

--- a/solution.py
+++ b/solution.py
@@ -15,6 +15,7 @@
 T = 128
 R = 160
 HALF = H // 2
+PARTS = ((0, H * FD), (H * FD, H * FD * 3 // 2), (H * FD * 3 // 2, 2 * H * FD))
 PAIR = 1.0 / math.sqrt(2.0 * FD)
 LINEAR = 1.0 / FD**0.25
 f32 = jnp.float32
@@ -83,7 +84,7 @@
     qt, kt, phi_q, phi_k, phi_qt, phi_kt, fold,
     score, a_low, value_part, den, g_low, gs, p_low, norm_t,
     span, contrib, other, pair_out, pair_in, chain_in, chain_out, back_out, back_in, pre, pre_out,
-    row_sum, query_sum, norm_own, norm_mate, norm_chip, norm_in, gden_t, dproj_t,
+    row_sum, query_sum, wg_t, norm_own, norm_mate, norm_chip, norm_in, gden_t, dproj_t,
     term, core_in, xs_out, xs_in, xz_out, xz_in, y_part, x_part,
     in_sem, out_sem,
     mate_send, mate_recv, norm_send, norm_recv, other_send, other_recv, pair_send, pair_recv,
@@ -95,8 +96,6 @@
     nz = ns // 2
     rows = d_model // ns
     pairs = nz // 2
-    half = H * FD
-    piece = half // nx
     dp = lax.axis_index("dp")
     me = lax.axis_index("seq")
     z, c = me // 2, lax.rem(me, 2)
@@ -190,31 +189,31 @@
 
     def core_copy(part, k):
         return remote(
-            term.at[part, 2 * k + (1 - c)], core_in.at[part, k],
+            term[part].at[2 * k + (1 - c)], core_in[part].at[k],
             core_send.at[part, k], core_recv.at[part, k], (dp, mate),
         )
 
     def xs_copy(part, step):
         return remote(
-            xs_out.at[part, x_peer(step)], xs_in.at[part, step],
+            xs_out[part].at[x_peer(step)], xs_in[part].at[step],
             xs_send.at[part, step], xs_recv.at[part, step], across_x(step),
         )
 
     def xz_copy(part, step):
         return remote(
-            xz_out.at[part, z_peer(step)], xz_in.at[part, step],
+            xz_out[part].at[z_peer(step)], xz_in[part].at[step],
             xz_send.at[part, step], xz_recv.at[part, step], across_z(step),
         )
 
     def y_copy(part, step, source):
         return remote(
-            y_part.at[part, source], y_part.at[part, source],
+            y_part[part].at[source], y_part[part].at[source],
             y_send.at[part, step], y_recv.at[part, step], across_y(step),
         )
 
     def x_copy(part, step, source):
         return remote(
-            x_part.at[part, source], x_part.at[part, source],
+            x_part[part].at[source], x_part[part].at[source],
             x_send.at[part, step], x_recv.at[part, step], across_x(step),
         )
 
@@ -397,21 +396,22 @@
     step_four(0)
 
     def send_terms(part):
-        left = dproj_t[part * half : (part + 1) * half, :].astype(bf16)
+        left = dproj_t[PARTS[part][0] : PARTS[part][1], :].astype(bf16)
         for k in range(nz):
             chunk = pl.ds(pl.multiple_of((2 * k + 1 - c) * rows, rows), rows)
-            term[part, 2 * k + 1 - c] = dot(left, tok[0, :, chunk])
+            term[part][2 * k + 1 - c] = dot(left, tok[0, :, chunk])
             core_copy(part, k).start()
         for k in range(nz):
             chunk = pl.ds(pl.multiple_of((2 * k + c) * rows, rows), rows)
-            term[part, 2 * k + c] = dot(left, tok[0, :, chunk])
+            term[part][2 * k + c] = dot(left, tok[0, :, chunk])
 
     def send_x(part):
         for k in range(nz):
             core_copy(part, k).wait_recv()
-            both = term[part, 2 * k + c] + core_in[part, k]
+            both = term[part][2 * k + c] + core_in[part][k]
+            piece = both.shape[0] // nx
             for j in range(nx):
-                xs_out[part, j, k] = both[j * piece : (j + 1) * piece]
+                xs_out[part][j, k] = both[j * piece : (j + 1) * piece]
         for step in range(1, nx):
             xs_copy(part, step).start()
 
@@ -419,36 +419,37 @@
         for step in range(1, nx):
             xs_copy(part, step).wait_recv()
         for k in range(nz):
-            acc = xs_out[part, x, k]
+            acc = xs_out[part][x, k]
             for step in range(1, nx):
-                acc = acc + xs_in[part, step, k]
-            xz_out[part, k] = acc
+                acc = acc + xs_in[part][step, k]
+            xz_out[part][k] = acc
         for step in range(1, nz):
             xz_copy(part, step).start()
 
     def send_y(part):
-        acc = xz_out[part, z]
+        acc = xz_out[part][z]
         for step in range(1, nz):
             xz_copy(part, step).wait_recv()
-            acc = acc + xz_in[part, step]
-        y_part[part, y] = acc
+            acc = acc + xz_in[part][step]
+        y_part[part][y] = acc
         for step in range(1, ny):
             y_copy(part, step, y).start()
 
     def send_all(part):
         for step in range(1, ny):
             y_copy(part, step, lax.rem(y + ny - step, ny)).wait_recv()
-        acc = y_part[part, 0]
+        acc = y_part[part][0]
         for j in range(1, ny):
-            acc = acc + y_part[part, j]
-        x_part[part, x] = acc * (1.0 / (ny * nx))
+            acc = acc + y_part[part][j]
+        x_part[part][x] = acc * (1.0 / (ny * nx))
         for step in range(1, nx):
             x_copy(part, step, x).start()
 
     def collect(part):
         for step in range(1, nx):
             x_copy(part, step, lax.rem(x + nx - step, nx)).wait_recv()
-        wg[:, part * half : (part + 1) * half] = x_part[part].reshape(half, rows).T
+        start, stop = PARTS[part]
+        wg_t[start:stop, :] = x_part[part][...].reshape(stop - start, rows)
 
     lane = lax.broadcasted_iota(jnp.int32, (T, DV), 1)
     gden_all = jnp.zeros((T, DV), f32)
@@ -507,9 +508,12 @@
         u = kt[feat(h), :]
         inner = dot(qt[feat(h), :].astype(bf16), gs[h])
         dproj_t[H * FD + h * FD : H * FD + (h + 1) * FD, :] = feature_grad(u, up) + inner
-    send_terms(1)
+        if h == HALF - 1:
+            send_terms(1)
+    send_terms(2)
     send_z(0)
     send_x(1)
+    send_x(2)
 
     for h in range(H):
         vg[0, :, lanes(h)] = (dot(a_low[h], g_low[h], 0, 0) + dot(phi_kt[h], p_low[h])).astype(bf16)
@@ -524,11 +528,16 @@
 
     send_y(0)
     send_z(1)
+    send_z(2)
     send_all(0)
     send_y(1)
+    send_y(2)
     collect(0)
     send_all(1)
+    send_all(2)
     collect(1)
+    collect(2)
+    wg[...] = wg_t[...].T
     store_wg = pltpu.make_async_copy(wg, wg_h, out_sem.at[2])
     store_wg.start()
 
@@ -548,7 +557,7 @@
             def _():
                 chain_copy(which, j).wait_send()
 
-    for part in range(2):
+    for part in range(len(PARTS)):
         for k in range(nz):
             core_copy(part, k).wait_send()
         for step in range(1, nz):
@@ -563,12 +572,19 @@
     store_wg.wait()
 
 
+def hand_over(*refs):
+    sems = refs[6]
+    copies = [pltpu.make_async_copy(refs[i], refs[3 + i], sems.at[i]) for i in range(3)]
+    for copy in copies:
+        copy.start()
+    for copy in copies:
+        copy.wait()
+
+
 def on_device(sizes, tokens, qk_weight, values, cotangent, key_span, key_norm, query_span, query_norm):
     ns, ny, nx, d_model = sizes
     nz = ns // 2
     rows = d_model // ns
-    half = H * FD
-    piece = half // nx
     width = 2 * H * FD
     key_span, query_span = (jnp.swapaxes(a, 2, 3) for a in (key_span, query_span))
     args = (tokens, qk_weight, values, cotangent, key_span, key_norm, query_span, query_norm)
@@ -578,6 +594,10 @@
         jax.ShapeDtypeStruct((rows, width), f32),
     )
     vmem, dma = pltpu.VMEM, pltpu.SemaphoreType.DMA
+
+    def each(shape):
+        return tuple(vmem(shape(stop - start), f32) for start, stop in PARTS)
+
     scratch = [vmem(a.shape, a.dtype) for a in args] + [vmem(o.shape, o.dtype) for o in out_shape]
     scratch += [
         vmem((H * FD, T), f32),
@@ -608,20 +628,21 @@
         vmem((2, HALF, R, DV), f32),
         vmem((R * H, DV), f32),
         vmem((R * H, DV), f32),
+        vmem((width, rows), f32),
         vmem((2, H, R), f32),
         vmem((2, H, R), f32),
         vmem((2, H, R), f32),
         vmem((2, nz, H, R), f32),
         vmem((H, T), f32),
         vmem((width, T), f32),
-        vmem((2, ns, half, rows), f32),
-        vmem((2, nz, half, rows), f32),
-        vmem((2, nx, nz, piece, rows), f32),
-        vmem((2, nx, nz, piece, rows), f32),
-        vmem((2, nz, piece, rows), f32),
-        vmem((2, nz, piece, rows), f32),
-        vmem((2, ny, piece, rows), f32),
-        vmem((2, nx, piece, rows), f32),
+        each(lambda n: (ns, n, rows)),
+        each(lambda n: (nz, n, rows)),
+        each(lambda n: (nx, nz, n // nx, rows)),
+        each(lambda n: (nx, nz, n // nx, rows)),
+        each(lambda n: (nz, n // nx, rows)),
+        each(lambda n: (nz, n // nx, rows)),
+        each(lambda n: (ny, n // nx, rows)),
+        each(lambda n: (nx, n // nx, rows)),
         dma((8,)), dma((3,)),
         dma((2,)), dma((2,)),
         dma((2, nz)), dma((2, nz)),
@@ -630,13 +651,13 @@
         dma((2, 2)), dma((2, 2)),
         dma((2, 2)), dma((2, 2)),
         dma((2, HALF)), dma((2, HALF)),
-        dma((2, nz)), dma((2, nz)),
-        dma((2, nx)), dma((2, nx)),
-        dma((2, nz)), dma((2, nz)),
-        dma((2, ny)), dma((2, ny)),
-        dma((2, nx)), dma((2, nx)),
+        dma((len(PARTS), nz)), dma((len(PARTS), nz)),
+        dma((len(PARTS), nx)), dma((len(PARTS), nx)),
+        dma((len(PARTS), nz)), dma((len(PARTS), nz)),
+        dma((len(PARTS), ny)), dma((len(PARTS), ny)),
+        dma((len(PARTS), nx)), dma((len(PARTS), nx)),
     ]
-    return pl.pallas_call(
+    results = pl.pallas_call(
         functools.partial(kernel, sizes),
         out_shape=out_shape,
         in_specs=[pl.BlockSpec(memory_space=pl.ANY)] * 8,
@@ -646,6 +667,13 @@
             collective_id=0, has_side_effects=True, vmem_limit_bytes=60 * 1024 * 1024
         ),
     )(*args)
+    return pl.pallas_call(
+        hand_over,
+        out_shape=out_shape,
+        in_specs=[pl.BlockSpec(memory_space=pl.ANY)] * 3,
+        out_specs=(pl.BlockSpec(memory_space=pl.ANY),) * 3,
+        scratch_shapes=[dma((3,))],
+    )(*results)
 
 
 def solution(mesh):

time: 90.2 us -> 115 us (1.27)
  Pallas kernels: 85.3 us -> 114 us
  local copies, waits for them, and re-layouts: 3.58 us -> 0 us
    pallas_call x0 -> x1, Pallas kernels: none -> 28.9 us  [on_device(): pl.pallas_call(hand_over, out_shape=out_shape, in_specs=[pl.BlockSpec(mem...]
    unnamed x7 -> x0, local copies, waits for them, and re-layouts: 3.58 us -> none
where the time goes in v4:
time: 115 us; the launch traced here: 114 us
  Pallas kernels  114 us (99%)
    pallas_call x1, Pallas kernels, on_device(): pl.pallas_call(functools.partial(kernel, sizes), out_shape=out_shape, in_...  84.9 us
    pallas_call x1, Pallas kernels, on_device(): pl.pallas_call(hand_over, out_shape=out_shape, in_specs=[pl.BlockSpec(mem...  28.9 us

profile of v4, /device:TPU:1, one launch (start us, length us, event | category | flops | bytes accessed | tf_op | source)
XLA Modules:
  0.0 114.4 jit_solution(12423820860407127359)
XLA Ops:
  0.6 84.9 %shard_map.103 = (bf16[1,128,2048]{2,1,0:T(8,128)(2,1)}, bf16[1,128,1024]{2,1,0:T(8,128)(2,1)}, f32[128,256]{1,0:T(8,128)}) custom-call(bf16[1,128,2048]{2,1,0:T(8,128)(2,1)} %tok_h.1, bf16[2048,256]{1,0:T(8,128)(2,1)} %w_h.1, bf16[1,128,1024]{2,1,0:T(8,128)(2,1)} %val_h.1, bf16[1,128,1024]{2,1,0:T(8,128)(2,1)} %cot_h.1, ...), custom_call_target="tpu_custom_call" | custom-call | tf_op jit(solution)/shard_map/pallas_call | solution.py:660
  85.5 28.9 %shard_map.104 = (bf16[1,128,2048]{2,1,0:T(8,128)(2,1)}, bf16[1,128,1024]{2,1,0:T(8,128)(2,1)}, f32[128,256]{1,0:T(8,128)}) custom-call(bf16[1,128,2048]{2,1,0:T(8,128)(2,1)} %get-tuple-element.6.refs_0_, bf16[1,128,1024]{2,1,0:T(8,128)(2,1)} %get-tuple-element.7.refs_1_, f32[128,256]{1,0:T(8,128)} %get-tuple-element.8.refs_2_), custom_call_target="tpu_custom_call" | custom-call | tf_op jit(solution)/shard_map/pallas_call | solution.py:670

commit v5 on v4

--- a/solution.py
+++ b/solution.py
@@ -15,7 +15,7 @@
 T = 128
 R = 160
 HALF = H // 2
-PARTS = ((0, H * FD), (H * FD, H * FD * 3 // 2), (H * FD * 3 // 2, 2 * H * FD))
+PARTS = ((0, H * FD), (H * FD, 2 * H * FD))
 PAIR = 1.0 / math.sqrt(2.0 * FD)
 LINEAR = 1.0 / FD**0.25
 f32 = jnp.float32
@@ -27,6 +27,10 @@
     return lax.dot_general(
         left, right, (((left_dim,), (right_dim,)), ((), ())), preferred_element_type=f32
     )
+
+
+def far_first(n):
+    return sorted(range(1, n), key=lambda step: -min(step, n - step))
 
 
 def split(x, parts):
@@ -187,10 +191,11 @@
             pre_send.at[which, k], pre_recv.at[which, k], (dp, mate),
         )
 
-    def core_copy(part, k):
-        return remote(
-            term[part].at[2 * k + (1 - c)], core_in[part].at[k],
-            core_send.at[part, k], core_recv.at[part, k], (dp, mate),
+    def core_copy(part, j):
+        run = pl.ds(j * (nz // 2), nz // 2)
+        return remote(
+            term[part].at[1 - c, run], core_in[part].at[run],
+            core_send.at[part, j], core_recv.at[part, j], (dp, mate),
         )
 
     def xs_copy(part, step):
@@ -279,7 +284,7 @@
         other_copy(0, k).start()
     mate_copy(0).wait_recv()
     norm_chip[0] = norm_own[0] + norm_mate[0]
-    for step in range(1, nz):
+    for step in far_first(nz):
         norm_copy(0, step).start()
 
     causal = lax.broadcasted_iota(jnp.int32, (T, T), 0) >= lax.broadcasted_iota(jnp.int32, (T, T), 1)
@@ -399,20 +404,22 @@
         left = dproj_t[PARTS[part][0] : PARTS[part][1], :].astype(bf16)
         for k in range(nz):
             chunk = pl.ds(pl.multiple_of((2 * k + 1 - c) * rows, rows), rows)
-            term[part][2 * k + 1 - c] = dot(left, tok[0, :, chunk])
-            core_copy(part, k).start()
+            term[part][1 - c, k] = dot(left, tok[0, :, chunk])
+            if k % (nz // 2) == nz // 2 - 1:
+                core_copy(part, k // (nz // 2)).start()
         for k in range(nz):
             chunk = pl.ds(pl.multiple_of((2 * k + c) * rows, rows), rows)
-            term[part][2 * k + c] = dot(left, tok[0, :, chunk])
+            term[part][c, k] = dot(left, tok[0, :, chunk])
 
     def send_x(part):
         for k in range(nz):
-            core_copy(part, k).wait_recv()
-            both = term[part][2 * k + c] + core_in[part][k]
+            if k % (nz // 2) == 0:
+                core_copy(part, k // (nz // 2)).wait_recv()
+            both = term[part][c, k] + core_in[part][k]
             piece = both.shape[0] // nx
             for j in range(nx):
                 xs_out[part][j, k] = both[j * piece : (j + 1) * piece]
-        for step in range(1, nx):
+        for step in far_first(nx):
             xs_copy(part, step).start()
 
     def send_z(part):
@@ -423,7 +430,7 @@
             for step in range(1, nx):
                 acc = acc + xs_in[part][step, k]
             xz_out[part][k] = acc
-        for step in range(1, nz):
+        for step in far_first(nz):
             xz_copy(part, step).start()
 
     def send_y(part):
@@ -432,7 +439,7 @@
             xz_copy(part, step).wait_recv()
             acc = acc + xz_in[part][step]
         y_part[part][y] = acc
-        for step in range(1, ny):
+        for step in far_first(ny):
             y_copy(part, step, y).start()
 
     def send_all(part):
@@ -442,7 +449,7 @@
         for j in range(1, ny):
             acc = acc + y_part[part][j]
         x_part[part][x] = acc * (1.0 / (ny * nx))
-        for step in range(1, nx):
+        for step in far_first(nx):
             x_copy(part, step, x).start()
 
     def collect(part):
@@ -472,7 +479,7 @@
     mate_copy(1).start()
     mate_copy(1).wait_recv()
     norm_chip[1] = norm_own[1] + norm_mate[1]
-    for step in range(1, nz):
+    for step in far_first(nz):
         norm_copy(1, step).start()
 
     high, low = split(gden_t[...], 2)
@@ -486,11 +493,15 @@
         u = qt[feat(h), :]
         dproj_t[feat(h), :] = feature_grad(u, up) + dot(kt[feat(h), :].astype(bf16), gs[h], 1, 1)
     send_terms(0)
-    send_x(0)
 
     @pl.when(early)
     def _():
         step_two(1)
+
+    send_x(0)
+
+    @pl.when(early)
+    def _():
         step_three(1)
 
     step_four(1)
@@ -508,12 +519,9 @@
         u = kt[feat(h), :]
         inner = dot(qt[feat(h), :].astype(bf16), gs[h])
         dproj_t[H * FD + h * FD : H * FD + (h + 1) * FD, :] = feature_grad(u, up) + inner
-        if h == HALF - 1:
-            send_terms(1)
-    send_terms(2)
+    send_terms(1)
     send_z(0)
     send_x(1)
-    send_x(2)
 
     for h in range(H):
         vg[0, :, lanes(h)] = (dot(a_low[h], g_low[h], 0, 0) + dot(phi_kt[h], p_low[h])).astype(bf16)
@@ -525,21 +533,6 @@
         tg[0, :, j * cols : (j + 1) * cols] = dot(dproj, w[j * cols : (j + 1) * cols, :], 1, 1).astype(bf16)
     store_tg = pltpu.make_async_copy(tg, tg_h, out_sem.at[1])
     store_tg.start()
-
-    send_y(0)
-    send_z(1)
-    send_z(2)
-    send_all(0)
-    send_y(1)
-    send_y(2)
-    collect(0)
-    send_all(1)
-    send_all(2)
-    collect(1)
-    collect(2)
-    wg[...] = wg_t[...].T
-    store_wg = pltpu.make_async_copy(wg, wg_h, out_sem.at[2])
-    store_wg.start()
 
     for which in range(2):
         mate_copy(which).wait_send()
@@ -557,28 +550,48 @@
             def _():
                 chain_copy(which, j).wait_send()
 
-    for part in range(len(PARTS)):
-        for k in range(nz):
-            core_copy(part, k).wait_send()
+    def sent(part):
+        for j in range(2):
+            core_copy(part, j).wait_send()
+        for step in range(1, nx):
+            xs_copy(part, step).wait_send()
         for step in range(1, nz):
             xz_copy(part, step).wait_send()
+
+    send_y(0)
+    sent(0)
+    send_z(1)
+    send_all(0)
+    send_y(1)
+    collect(0)
+    sent(1)
+    store_vg.wait()
+    store_tg.wait()
+    send_all(1)
+    for part in range(len(PARTS)):
         for step in range(1, ny):
             y_copy(part, step, y).wait_send()
+    collect(1)
+    wg[...] = wg_t[...].T
+    store_wg = pltpu.make_async_copy(wg, wg_h, out_sem.at[2])
+    store_wg.start()
+    for part in range(len(PARTS)):
         for step in range(1, nx):
-            xs_copy(part, step).wait_send()
             x_copy(part, step, x).wait_send()
-    store_vg.wait()
-    store_tg.wait()
     store_wg.wait()
 
 
 def hand_over(*refs):
-    sems = refs[6]
-    copies = [pltpu.make_async_copy(refs[i], refs[3 + i], sems.at[i]) for i in range(3)]
-    for copy in copies:
-        copy.start()
-    for copy in copies:
-        copy.wait()
+    held, load_sem, store_sem = refs[6:9], refs[9], refs[10]
+    loads = [pltpu.make_async_copy(refs[i], held[i], load_sem.at[i]) for i in range(3)]
+    stores = [pltpu.make_async_copy(held[i], refs[3 + i], store_sem.at[i]) for i in range(3)]
+    for load in loads:
+        load.start()
+    for load, store in zip(loads, stores):
+        load.wait()
+        store.start()
+    for store in stores:
+        store.wait()
 
 
 def on_device(sizes, tokens, qk_weight, values, cotangent, key_span, key_norm, query_span, query_norm):
@@ -635,7 +648,7 @@
         vmem((2, nz, H, R), f32),
         vmem((H, T), f32),
         vmem((width, T), f32),
-        each(lambda n: (ns, n, rows)),
+        each(lambda n: (2, nz, n, rows)),
         each(lambda n: (nz, n, rows)),
         each(lambda n: (nx, nz, n // nx, rows)),
         each(lambda n: (nx, nz, n // nx, rows)),
@@ -651,7 +664,7 @@
         dma((2, 2)), dma((2, 2)),
         dma((2, 2)), dma((2, 2)),
         dma((2, HALF)), dma((2, HALF)),
-        dma((len(PARTS), nz)), dma((len(PARTS), nz)),
+        dma((len(PARTS), 2)), dma((len(PARTS), 2)),
         dma((len(PARTS), nx)), dma((len(PARTS), nx)),
         dma((len(PARTS), nz)), dma((len(PARTS), nz)),
         dma((len(PARTS), ny)), dma((len(PARTS), ny)),
@@ -672,7 +685,7 @@
         out_shape=out_shape,
         in_specs=[pl.BlockSpec(memory_space=pl.ANY)] * 3,
         out_specs=(pl.BlockSpec(memory_space=pl.ANY),) * 3,
-        scratch_shapes=[dma((3,))],
+        scratch_shapes=[vmem(o.shape, o.dtype) for o in out_shape] + [dma((3,)), dma((3,))],
     )(*results)
 
 

time: 115 us -> 86.5 us (0.75)
  Pallas kernels: 114 us -> 84.8 us
    pallas_call x1, Pallas kernels: 28.9 us -> 2.01 us  [on_device(): pl.pallas_call(hand_over, out_shape=out_shape, in_specs=[pl.BlockSpec(mem...]
    pallas_call x1, Pallas kernels: 84.9 us -> 82.8 us  [on_device(): pl.pallas_call(functools.partial(kernel, sizes), out_shape=out_shape, in_...]
where the time goes in v5:
time: 86.5 us; the launch traced here: 85.4 us
  Pallas kernels  84.8 us (98%)
    pallas_call x1, Pallas kernels, on_device(): pl.pallas_call(functools.partial(kernel, sizes), out_shape=out_shape, in_...  82.8 us
    pallas_call x1, Pallas kernels, on_device(): pl.pallas_call(hand_over, out_shape=out_shape, in_specs=[pl.BlockSpec(mem...  2.01 us

profile of v5, /device:TPU:1, one launch (start us, length us, event | category | flops | bytes accessed | tf_op | source)
XLA Modules:
  0.0 85.4 jit_solution(11358095672780791866)
XLA Ops:
  0.6 82.8 %shard_map.103 = (bf16[1,128,2048]{2,1,0:T(8,128)(2,1)}, bf16[1,128,1024]{2,1,0:T(8,128)(2,1)}, f32[128,256]{1,0:T(8,128)}) custom-call(bf16[1,128,2048]{2,1,0:T(8,128)(2,1)} %tok_h.1, bf16[2048,256]{1,0:T(8,128)(2,1)} %w_h.1, bf16[1,128,1024]{2,1,0:T(8,128)(2,1)} %val_h.1, bf16[1,128,1024]{2,1,0:T(8,128)(2,1)} %cot_h.1, ...), custom_call_target="tpu_custom_call" | custom-call | tf_op jit(solution)/shard_map/pallas_call | solution.py:673
  83.4 2.0 %shard_map.104 = (bf16[1,128,2048]{2,1,0:T(8,128)(2,1)}, bf16[1,128,1024]{2,1,0:T(8,128)(2,1)}, f32[128,256]{1,0:T(8,128)}) custom-call(bf16[1,128,2048]{2,1,0:T(8,128)(2,1)} %get-tuple-element.6.refs_0_, bf16[1,128,1024]{2,1,0:T(8,128)(2,1)} %get-tuple-element.7.refs_1_, f32[128,256]{1,0:T(8,128)} %get-tuple-element.8.refs_2_), custom_call_target="tpu_custom_call" | custom-call | tf_op jit(solution)/shard_map/pallas_call | solution.py:683

commit v6 on v5

--- a/solution.py
+++ b/solution.py
@@ -520,8 +520,8 @@
         inner = dot(qt[feat(h), :].astype(bf16), gs[h])
         dproj_t[H * FD + h * FD : H * FD + (h + 1) * FD, :] = feature_grad(u, up) + inner
     send_terms(1)
+    send_x(1)
     send_z(0)
-    send_x(1)
 
     for h in range(H):
         vg[0, :, lanes(h)] = (dot(a_low[h], g_low[h], 0, 0) + dot(phi_kt[h], p_low[h])).astype(bf16)
@@ -558,16 +558,16 @@
         for step in range(1, nz):
             xz_copy(part, step).wait_send()
 
+    send_z(1)
     send_y(0)
     sent(0)
-    send_z(1)
+    send_y(1)
     send_all(0)
-    send_y(1)
-    collect(0)
     sent(1)
     store_vg.wait()
     store_tg.wait()
     send_all(1)
+    collect(0)
     for part in range(len(PARTS)):
         for step in range(1, ny):
             y_copy(part, step, y).wait_send()

time: 86.5 us -> 84 us (0.971)
  Pallas kernels: 84.8 us -> 82.3 us
    pallas_call x1, Pallas kernels: 82.8 us -> 80.3 us  [on_device(): pl.pallas_call(functools.partial(kernel, sizes), out_shape=out_shape, in_...]
where the time goes in v6:
time: 84 us; the launch traced here: 83 us
  Pallas kernels  82.3 us (98%)
    pallas_call x1, Pallas kernels, on_device(): pl.pallas_call(functools.partial(kernel, sizes), out_shape=out_shape, in_...  80.3 us
    pallas_call x1, Pallas kernels, on_device(): pl.pallas_call(hand_over, out_shape=out_shape, in_specs=[pl.BlockSpec(mem...  2.01 us

profile of v6, /device:TPU:1, one launch (start us, length us, event | category | flops | bytes accessed | tf_op | source)
XLA Modules:
  0.0 83.0 jit_solution(9379152601694255202)
XLA Ops:
  0.6 80.3 %shard_map.103 = (bf16[1,128,2048]{2,1,0:T(8,128)(2,1)}, bf16[1,128,1024]{2,1,0:T(8,128)(2,1)}, f32[128,256]{1,0:T(8,128)}) custom-call(bf16[1,128,2048]{2,1,0:T(8,128)(2,1)} %tok_h.1, bf16[2048,256]{1,0:T(8,128)(2,1)} %w_h.1, bf16[1,128,1024]{2,1,0:T(8,128)(2,1)} %val_h.1, bf16[1,128,1024]{2,1,0:T(8,128)(2,1)} %cot_h.1, ...), custom_call_target="tpu_custom_call" | custom-call | tf_op jit(solution)/shard_map/pallas_call | solution.py:673
  81.0 2.0 %shard_map.104 = (bf16[1,128,2048]{2,1,0:T(8,128)(2,1)}, bf16[1,128,1024]{2,1,0:T(8,128)(2,1)}, f32[128,256]{1,0:T(8,128)}) custom-call(bf16[1,128,2048]{2,1,0:T(8,128)(2,1)} %get-tuple-element.6.refs_0_, bf16[1,128,1024]{2,1,0:T(8,128)(2,1)} %get-tuple-element.7.refs_1_, f32[128,256]{1,0:T(8,128)} %get-tuple-element.8.refs_2_), custom_call_target="tpu_custom_call" | custom-call | tf_op jit(solution)/shard_map/pallas_call | solution.py:683

commit v7 on v6

--- a/solution.py
+++ b/solution.py
@@ -198,10 +198,11 @@
             core_send.at[part, j], core_recv.at[part, j], (dp, mate),
         )
 
-    def xs_copy(part, step):
-        return remote(
-            xs_out[part].at[x_peer(step)], xs_in[part].at[step],
-            xs_send.at[part, step], xs_recv.at[part, step], across_x(step),
+    def xs_copy(part, step, group):
+        run = pl.ds(group * (nz // 2), nz // 2)
+        return remote(
+            xs_out[part].at[x_peer(step), run], xs_in[part].at[step, run],
+            xs_send.at[part, group, step], xs_recv.at[part, group, step], across_x(step),
         )
 
     def xz_copy(part, step):
@@ -412,26 +413,29 @@
             term[part][c, k] = dot(left, tok[0, :, chunk])
 
     def send_x(part):
-        for k in range(nz):
-            if k % (nz // 2) == 0:
-                core_copy(part, k // (nz // 2)).wait_recv()
-            both = term[part][c, k] + core_in[part][k]
-            piece = both.shape[0] // nx
-            for j in range(nx):
-                xs_out[part][j, k] = both[j * piece : (j + 1) * piece]
-        for step in far_first(nx):
-            xs_copy(part, step).start()
+        for group in range(2):
+            core_copy(part, group).wait_recv()
+            for k in range(group * (nz // 2), (group + 1) * (nz // 2)):
+                both = term[part][c, k] + core_in[part][k]
+                piece = both.shape[0] // nx
+                for j in range(nx):
+                    xs_out[part][j, k] = both[j * piece : (j + 1) * piece]
+            for step in far_first(nx):
+                xs_copy(part, step, group).start()
 
     def send_z(part):
-        for step in range(1, nx):
-            xs_copy(part, step).wait_recv()
-        for k in range(nz):
-            acc = xs_out[part][x, k]
+        for group in range(2):
             for step in range(1, nx):
-                acc = acc + xs_in[part][step, k]
-            xz_out[part][k] = acc
-        for step in far_first(nz):
-            xz_copy(part, step).start()
+                xs_copy(part, step, group).wait_recv()
+            for k in range(group * (nz // 2), (group + 1) * (nz // 2)):
+                acc = xs_out[part][x, k]
+                for step in range(1, nx):
+                    acc = acc + xs_in[part][step, k]
+                xz_out[part][k] = acc
+
+                @pl.when(k != z)
+                def _():
+                    xz_copy(part, lax.rem(k + nz - z, nz)).start()
 
     def send_y(part):
         acc = xz_out[part][z]
@@ -554,7 +558,8 @@
         for j in range(2):
             core_copy(part, j).wait_send()
         for step in range(1, nx):
-            xs_copy(part, step).wait_send()
+            for group in range(2):
+                xs_copy(part, step, group).wait_send()
         for step in range(1, nz):
             xz_copy(part, step).wait_send()
 
@@ -665,7 +670,7 @@
         dma((2, 2)), dma((2, 2)),
         dma((2, HALF)), dma((2, HALF)),
         dma((len(PARTS), 2)), dma((len(PARTS), 2)),
-        dma((len(PARTS), nx)), dma((len(PARTS), nx)),
+        dma((len(PARTS), 2, nx)), dma((len(PARTS), 2, nx)),
         dma((len(PARTS), nz)), dma((len(PARTS), nz)),
         dma((len(PARTS), ny)), dma((len(PARTS), ny)),
         dma((len(PARTS), nx)), dma((len(PARTS), nx)),

time: 84 us -> 81.2 us (0.967)
  Pallas kernels: 82.3 us -> 79.8 us
    pallas_call x1, Pallas kernels: 80.3 us -> 77.8 us  [on_device(): pl.pallas_call(functools.partial(kernel, sizes), out_shape=out_shape, in_...]
where the time goes in v7:
time: 81.2 us; the launch traced here: 80.4 us
  Pallas kernels  79.8 us (98%)
    pallas_call x1, Pallas kernels, on_device(): pl.pallas_call(functools.partial(kernel, sizes), out_shape=out_shape, in_...  77.8 us
    pallas_call x1, Pallas kernels, on_device(): pl.pallas_call(hand_over, out_shape=out_shape, in_specs=[pl.BlockSpec(mem...  2.01 us

profile of v7, /device:TPU:1, one launch (start us, length us, event | category | flops | bytes accessed | tf_op | source)
XLA Modules:
  0.0 80.4 jit_solution(11662346075695520039)
XLA Ops:
  0.6 77.8 %shard_map.103 = (bf16[1,128,2048]{2,1,0:T(8,128)(2,1)}, bf16[1,128,1024]{2,1,0:T(8,128)(2,1)}, f32[128,256]{1,0:T(8,128)}) custom-call(bf16[1,128,2048]{2,1,0:T(8,128)(2,1)} %tok_h.1, bf16[2048,256]{1,0:T(8,128)(2,1)} %w_h.1, bf16[1,128,1024]{2,1,0:T(8,128)(2,1)} %val_h.1, bf16[1,128,1024]{2,1,0:T(8,128)(2,1)} %cot_h.1, ...), custom_call_target="tpu_custom_call" | custom-call | tf_op jit(solution)/shard_map/pallas_call | solution.py:678
  78.4 2.0 %shard_map.104 = (bf16[1,128,2048]{2,1,0:T(8,128)(2,1)}, bf16[1,128,1024]{2,1,0:T(8,128)(2,1)}, f32[128,256]{1,0:T(8,128)}) custom-call(bf16[1,128,2048]{2,1,0:T(8,128)(2,1)} %get-tuple-element.6.refs_0_, bf16[1,128,1024]{2,1,0:T(8,128)(2,1)} %get-tuple-element.7.refs_1_, f32[128,256]{1,0:T(8,128)} %get-tuple-element.8.refs_2_), custom_call_target="tpu_custom_call" | custom-call | tf_op jit(solution)/shard_map/pallas_call | solution.py:688

commit v8 on v7

--- a/solution.py
+++ b/solution.py
@@ -100,6 +100,8 @@
     nz = ns // 2
     rows = d_model // ns
     pairs = nz // 2
+    groups = min(4, nz)
+    run_len = nz // groups
     dp = lax.axis_index("dp")
     me = lax.axis_index("seq")
     z, c = me // 2, lax.rem(me, 2)
@@ -192,14 +194,14 @@
         )
 
     def core_copy(part, j):
-        run = pl.ds(j * (nz // 2), nz // 2)
+        run = pl.ds(j * run_len, run_len)
         return remote(
             term[part].at[1 - c, run], core_in[part].at[run],
             core_send.at[part, j], core_recv.at[part, j], (dp, mate),
         )
 
     def xs_copy(part, step, group):
-        run = pl.ds(group * (nz // 2), nz // 2)
+        run = pl.ds(group * run_len, run_len)
         return remote(
             xs_out[part].at[x_peer(step), run], xs_in[part].at[step, run],
             xs_send.at[part, group, step], xs_recv.at[part, group, step], across_x(step),
@@ -406,16 +408,16 @@
         for k in range(nz):
             chunk = pl.ds(pl.multiple_of((2 * k + 1 - c) * rows, rows), rows)
             term[part][1 - c, k] = dot(left, tok[0, :, chunk])
-            if k % (nz // 2) == nz // 2 - 1:
-                core_copy(part, k // (nz // 2)).start()
+            if k % run_len == run_len - 1:
+                core_copy(part, k // run_len).start()
         for k in range(nz):
             chunk = pl.ds(pl.multiple_of((2 * k + c) * rows, rows), rows)
             term[part][c, k] = dot(left, tok[0, :, chunk])
 
     def send_x(part):
-        for group in range(2):
+        for group in range(groups):
             core_copy(part, group).wait_recv()
-            for k in range(group * (nz // 2), (group + 1) * (nz // 2)):
+            for k in range(group * run_len, (group + 1) * run_len):
                 both = term[part][c, k] + core_in[part][k]
                 piece = both.shape[0] // nx
                 for j in range(nx):
@@ -424,10 +426,10 @@
                 xs_copy(part, step, group).start()
 
     def send_z(part):
-        for group in range(2):
+        for group in range(groups):
             for step in range(1, nx):
                 xs_copy(part, step, group).wait_recv()
-            for k in range(group * (nz // 2), (group + 1) * (nz // 2)):
+            for k in range(group * run_len, (group + 1) * run_len):
                 acc = xs_out[part][x, k]
                 for step in range(1, nx):
                     acc = acc + xs_in[part][step, k]
@@ -555,10 +557,10 @@
                 chain_copy(which, j).wait_send()
 
     def sent(part):
-        for j in range(2):
+        for j in range(groups):
             core_copy(part, j).wait_send()
         for step in range(1, nx):
-            for group in range(2):
+            for group in range(groups):
                 xs_copy(part, step, group).wait_send()
         for step in range(1, nz):
             xz_copy(part, step).wait_send()
@@ -669,8 +671,8 @@
         dma((2, 2)), dma((2, 2)),
         dma((2, 2)), dma((2, 2)),
         dma((2, HALF)), dma((2, HALF)),
-        dma((len(PARTS), 2)), dma((len(PARTS), 2)),
-        dma((len(PARTS), 2, nx)), dma((len(PARTS), 2, nx)),
+        dma((len(PARTS), min(4, nz))), dma((len(PARTS), min(4, nz))),
+        dma((len(PARTS), min(4, nz), nx)), dma((len(PARTS), min(4, nz), nx)),
         dma((len(PARTS), nz)), dma((len(PARTS), nz)),
         dma((len(PARTS), ny)), dma((len(PARTS), ny)),
         dma((len(PARTS), nx)), dma((len(PARTS), nx)),

time: 81.2 us -> 81.1 us (level)
  Pallas kernels: 79.8 us -> 78.9 us
    pallas_call x1, Pallas kernels: 77.8 us -> 76.9 us  [on_device(): pl.pallas_call(functools.partial(kernel, sizes), out_shape=out_shape, in_...]
where the time goes in v8:
time: 81.1 us; the launch traced here: 79.5 us
  Pallas kernels  78.9 us (97%)
    pallas_call x1, Pallas kernels, on_device(): pl.pallas_call(functools.partial(kernel, sizes), out_shape=out_shape, in_...  76.9 us
    pallas_call x1, Pallas kernels, on_device(): pl.pallas_call(hand_over, out_shape=out_shape, in_specs=[pl.BlockSpec(mem...  2.01 us

profile of v8, /device:TPU:1, one launch (start us, length us, event | category | flops | bytes accessed | tf_op | source)
XLA Modules:
  0.0 79.5 jit_solution(7168673523190587790)
XLA Ops:
  0.6 76.9 %shard_map.103 = (bf16[1,128,2048]{2,1,0:T(8,128)(2,1)}, bf16[1,128,1024]{2,1,0:T(8,128)(2,1)}, f32[128,256]{1,0:T(8,128)}) custom-call(bf16[1,128,2048]{2,1,0:T(8,128)(2,1)} %tok_h.1, bf16[2048,256]{1,0:T(8,128)(2,1)} %w_h.1, bf16[1,128,1024]{2,1,0:T(8,128)(2,1)} %val_h.1, bf16[1,128,1024]{2,1,0:T(8,128)(2,1)} %cot_h.1, ...), custom_call_target="tpu_custom_call" | custom-call | tf_op jit(solution)/shard_map/pallas_call | solution.py:680
  77.5 2.0 %shard_map.104 = (bf16[1,128,2048]{2,1,0:T(8,128)(2,1)}, bf16[1,128,1024]{2,1,0:T(8,128)(2,1)}, f32[128,256]{1,0:T(8,128)}) custom-call(bf16[1,128,2048]{2,1,0:T(8,128)(2,1)} %get-tuple-element.6.refs_0_, bf16[1,128,1024]{2,1,0:T(8,128)(2,1)} %get-tuple-element.7.refs_1_, f32[128,256]{1,0:T(8,128)} %get-tuple-element.8.refs_2_), custom_call_target="tpu_custom_call" | custom-call | tf_op jit(solution)/shard_map/pallas_call | solution.py:690
